TPU v7x, 1024 devices: a whole 4x8x16 slice. The times are simulated.
1024 devices in a mesh: wave: 128 (over y, z), ocean: 8 (over x, core).
Axes of the slice: x: 4, y: 8, z: 16, core: 2. Of those that a mesh axis runs over, the one named last changes fastest.
Arguments:
- spectra: float32 [128, 36, 36, 1024], P('wave', None, None, 'ocean'), may hold values from 0.2 to 2, as said below
- surface_wind: float32 [2, 128, 1024], P(None, 'wave', 'ocean'), may hold values from -6.5 to 6.5
- water_mask: int32 [128, 1024], P('wave', 'ocean'), may hold values 0 or 1
- send_rows: int32 [8, 65536], P(None, ('wave', 'ocean')), may hold values from 0 to 127, as said below
- send_count: int32 [8, 1024], P(None, ('wave', 'ocean')), may hold values from 8 to 64, as said below
- pick_slot: int32 [4, 524288], P(None, ('wave', 'ocean')), may hold values from 0 to 511, as said below
- pick_weight: float32 [4, 524288], P(None, ('wave', 'ocean')), may hold values from 0.05 to 0.5
- ocean_current: float32 [2, 524288], P(None, ('wave', 'ocean')), may hold values from -4 to 4
Outputs:
- ocean_forcing: float32 [34, 524288], P(None, ('wave', 'ocean'))
- wave_current: float32 [2, 128, 1024], P(None, 'wave', 'ocean')
Inputs may be any that keep to these rules, and one draw needn't show every extreme that they name: `spectra`: energy density of each spectral bin. `send_rows`: indices of the sending device's own wave points, numbered row-major over its 1 x 128 block. `send_count`: in every strip one owner receives 64 live rows from every device of the strip. `pick_slot`: source owner times 64 plus a slot below that source's live count toward this device.
All inputs are finite; a program needn't handle non-finite values. No bound on the sum of `water_mask` on one device may be relied on, other than what follows from the above.
Results may differ from a plain program's by a relative error of at most 0.0003.
Values sent between devices are 32-bit elements; how exact they have to be, the bound alone decides.
A program may use at most 32 MiB of HBM per device.

v0:
```python
import jax
import jax.numpy as jnp
from jax import lax
from jax.sharding import PartitionSpec as P

ND = 36
NF = 36
DEPTHS = 16


def with_halo(cells, sides, width):
    for axis, dim in sides:
        count = lax.axis_size(axis)
        ends = count - 1
        head = lax.slice_in_dim(cells, 0, width, axis=dim)
        tail = lax.slice_in_dim(cells, cells.shape[dim] - width, cells.shape[dim], axis=dim)
        cells = jnp.concatenate(
            [
                lax.ppermute(tail, axis, [(i, (i + 1) % count) for i in range(ends)]),
                cells,
                lax.ppermute(head, axis, [((i + 1) % count, i) for i in range(ends)]),
            ],
            axis=dim,
        )
    return cells


def tables():
    headings = jnp.arange(ND, dtype=jnp.float32)
    angles = (headings + 0.5) * (2.0 * jnp.pi / ND)
    cosine = jnp.cos(angles)
    sines = jnp.sin(angles)
    frequency = jnp.arange(NF, dtype=jnp.float32)
    speeds = 0.7 * jnp.power(1.1, -frequency)
    ratios = jnp.power(1.1, frequency - (NF - 1))
    kappas = 0.02 * jnp.power(1.1, 2.0 * frequency)
    depths = 0.25 * jnp.arange(DEPTHS, dtype=jnp.float32)
    kernel = jnp.sqrt(kappas)[:, None] * jnp.exp(-2.0 * kappas[:, None] * depths[None, :])
    return (cosine, sines, speeds, ratios, kernel)


def driving(surface_wind, cosine, sines):
    return jax.nn.relu(
        surface_wind[0][:, None, None, :] * cosine[None, :, None, None]
        + surface_wind[1][:, None, None, :] * sines[None, :, None, None]
    )


def advance(padded, surface_wind, ocean_cells, cosine, sines, speeds, ratios):
    centre = padded[1:-1, :, :, 1:-1]
    behind_x = padded[:-2, :, :, 1:-1]
    ahead_x = padded[2:, :, :, 1:-1]
    behind_y = padded[1:-1, :, :, :-2]
    ahead_y = padded[1:-1, :, :, 2:]
    along_x = (cosine[:, None] * speeds[None, :])[None, :, :, None]
    along_y = (sines[:, None] * speeds[None, :])[None, :, :, None]
    advected = (
        centre
        - jnp.maximum(along_x, 0.0) * (centre - behind_x)
        - jnp.minimum(along_x, 0.0) * (ahead_x - centre)
        - jnp.maximum(along_y, 0.0) * (centre - behind_y)
        - jnp.minimum(along_y, 0.0) * (ahead_y - centre)
    )
    energy = jnp.mean(advected, axis=(1, 2), keepdims=True)
    rates = ratios[None, None, :, None]
    factor = (
        1.0
        + 0.1 * rates * driving(surface_wind, cosine, sines)
        - 0.3 * rates * energy / (energy + 1.0)
    )
    return ocean_cells[:, None, None, :] * advected * factor


def project(spectrum, surface_wind, cosine, sines, ratios, kernel):
    weights_s = (
        jnp.concatenate(
            [cosine[:, None, None] * kernel[None], sines[:, None, None] * kernel[None]], 2
        )
        / ND
    )
    stokes = jnp.einsum("xdfy,dfc->cxy", spectrum, weights_s, precision=lax.Precision.HIGHEST)
    pushed = spectrum * (0.1 * ratios[None, None, :, None]) * driving(surface_wind, cosine, sines)
    compass = jnp.stack([cosine, sines], 1) / ND
    stress = jnp.einsum("xdfy,dc->cxy", pushed, compass, precision=lax.Precision.HIGHEST)
    return jnp.concatenate([stokes, stress], 0)


def pack_rows(column_collection, row_ids, number_of_rows):
    owners, slot_grand_sum = row_ids.shape
    active_flag = (
        jnp.arange(slot_grand_sum, dtype=jnp.int32)[None, :] < number_of_rows[:, None]
    ).astype(jnp.float32)
    collected_values = jnp.take(column_collection, row_ids.reshape(-1), axis=1).reshape(
        column_collection.shape[0], owners, slot_grand_sum
    )
    return collected_values * active_flag[None]


def blend_slots(received, picked, weights):
    values = jnp.take(received, picked.reshape(-1), axis=1).reshape(
        received.shape[0], picked.shape[0], picked.shape[1]
    )
    return jnp.sum(values * weights[None], axis=1)


def spread_values(current, picked, weights, slot_grand_sum):
    carried = jnp.concatenate([current, jnp.ones((1, current.shape[1]), jnp.float32)], 0)
    weighted = (carried[:, None, :] * weights[None]).reshape(3, -1)
    return jnp.zeros((3, slot_grand_sum), jnp.float32).at[:, picked.reshape(-1)].add(weighted)


def settle(returned, row_ids, points):
    totals = (
        jnp.zeros((3, points), jnp.float32).at[:, row_ids.reshape(-1)].add(returned.reshape(3, -1))
    )
    return totals[:2] / jnp.maximum(totals[2:], 1.0)


def per_device(
    spectra, surface_wind, water_mask, send_rows, send_count, pick_slot, pick_weight, ocean_current
):
    cosine, sines, speeds, ratios, kernel = tables()
    ocean_cells = water_mask.astype(jnp.float32)
    strip_rows, headings_n, freq_n, strip_cols = spectra.shape
    spectrum = spectra
    for sweep in range(2):
        padded = with_halo(spectrum, (("wave", 0), ("ocean", 3)), 1)
        spectrum = advance(padded, surface_wind, ocean_cells, cosine, sines, speeds, ratios)
    fields = project(spectrum, surface_wind, cosine, sines, ratios, kernel)
    channels = fields.shape[0]
    points = strip_rows * strip_cols
    flattened = fields.reshape(channels, points)
    owners, slot_grand_sum = send_rows.shape
    every_field, every_row, every_count = (
        lax.all_gather(flattened[None], "ocean", axis=0, tiled=True),
        lax.all_gather(send_rows[None], "ocean", axis=0, tiled=True),
        lax.all_gather(send_count.reshape(1, owners), "ocean", axis=0, tiled=True),
    )
    owner_index = lax.axis_index("ocean")
    mine_rows = lax.dynamic_index_in_dim(every_row, owner_index, 1, keepdims=False)
    mine_count = lax.dynamic_index_in_dim(every_count, owner_index, 1, keepdims=False)
    sources = jax.vmap(pack_rows)(every_field, mine_rows[:, None, :], mine_count[:, None])
    received = (
        sources.reshape(owners, channels, slot_grand_sum)
        .transpose(1, 0, 2)
        .reshape(channels, owners * slot_grand_sum)
    )
    ocean_forcing = blend_slots(received, pick_slot, pick_weight)
    slot_sums = spread_values(ocean_current, pick_slot, pick_weight, owners * slot_grand_sum)
    returned = lax.all_to_all(
        slot_sums.reshape(3, owners, slot_grand_sum),
        "ocean",
        split_axis=1,
        concat_axis=1,
        tiled=True,
    )
    wave_current = settle(returned, send_rows, points)
    return (ocean_forcing, wave_current.reshape(2, strip_rows, strip_cols))


def solution(mesh):
    in_specs = (
        P("wave", None, None, "ocean"),
        P(None, "wave", "ocean"),
        P("wave", "ocean"),
        P(None, ("wave", "ocean")),
        P(None, ("wave", "ocean")),
        P(None, ("wave", "ocean")),
        P(None, ("wave", "ocean")),
        P(None, ("wave", "ocean")),
    )
    out_specs = (P(None, ("wave", "ocean")), P(None, "wave", "ocean"))
    return jax.shard_map(
        per_device, mesh=mesh, in_specs=in_specs, out_specs=out_specs, check_vma=False
    )
```

profile of v0, /device:TPU:33, one launch (start us, length us, event | category | flops | bytes accessed | tf_op | source)
XLA Modules:
  0.0 165.0 jit_solution(11735547772631148914)
XLA Ops:
  2.7 4.1 %collective-permute-start = (f32[1,36,36,128]{3,2,1,0:T(8,128)}, f32[1,36,36,128]{3,2,1,0:T(8,128)}, u32[]{:S(2)}, u32[]{:S(2)}) collective-permute-start(f32[1,36,36,128]{3,2,1,0:T(8,128)} %copy.75), channel_id=1, source_target_pairs={{0,8},{8,16},{16,24},{24,32},{32,40},{40,48},{48,56},{56,64},{64,7... | collective-permute-start | bytes 1990664 | tf_op jit(solution)/shard_map/ppermute | solution.py:19
  6.8 15.8 %collective-permute-start.1 = (f32[1,36,36,128]{3,2,1,0:T(8,128)}, f32[1,36,36,128]{3,2,1,0:T(8,128)}, u32[]{:S(2)}, u32[]{:S(2)}) collective-permute-start(f32[1,36,36,128]{3,2,1,0:T(8,128)} %copy.75), channel_id=1, source_target_pairs={{8,0},{16,8},{24,16},{32,24},{40,32},{48,40},{56,48},{64,56},{72,6... | collective-permute-start | bytes 1990664 | tf_op jit(solution)/shard_map/ppermute | solution.py:21
  25.2 11.6 %scatter_custom_fusion = f32[3,512]{0,1:T(8,128)S(1)} fusion(s32[2048]{0:T(1024)S(1)} %bitcast.63, f32[3,2048]{0,1:T(8,128)S(1)} %bitcast_multiply_fusion, f32[]{:T(128)} %constant.53.clone.1), kind=kCustom, calls=%fused_computation.7 | custom fusion | flops 6144 | bytes 1054724 | tf_op jit(solution)/shard_map/scatter-add | solution.py:109
  37.6 5.3 %all-to-all-start = ((f32[8,1,192]{2,1,0:T(1,128)}), f32[8,1,192]{2,1,0:T(1,128)S(1)}, u32[]{:S(2)}, u32[]{:S(2)}) async-start(f32[8,1,192]{2,1,0:T(1,128)} %reshape.704), calls=%async_computation | async-start | bytes 16384 | tf_op jit(solution)/shard_map/all_to_all | solution.py:150
  43.1 13.5 %all-gather = s32[64,64]{1,0:T(8,128)S(1)} all-gather(s32[8,64]{1,0:T(8,128)S(1)} %copy-done.6), channel_id=2, replica_groups=mesh['wave'=128,'ocean'=8] {'ocean'}, dimensions={0}, use_global_device_ids=true | all-gather | bytes 18432 | tf_op jit(solution)/shard_map/all_gather | solution.py:136
  59.3 7.1 %all-reduce.2 = s32[8,8]{1,0:T(8,128)S(1)} all-reduce(s32[8,8]{1,0:T(8,128)S(1)} %reshape.681), channel_id=4, replica_groups=mesh['wave'=128,'ocean'=8] {'ocean'}, use_global_device_ids=true, to_apply=%add.1 | all-reduce | flops 64 | bytes 512
  69.3 2.7 %fusion.52 = (f32[3,36,36,1]{3,2,1,0:T(8,128)}, f32[3,36,36,1]{3,2,1,0:T(8,128)}) fusion(f32[3,36,36,128]{3,2,1,0:T(8,128)S(1)} %constant_dynamic-update-slice_fusion), kind=kLoop, calls=%fused_computation.116 | loop fusion | bytes 62208 | tf_op jit(solution)/shard_map/slice | solution.py:16
  72.0 2.5 %copy.79 = f32[3,36,36,1]{2,1,3,0:T(8,128)S(1)} copy(f32[3,36,36,1]{3,2,1,0:T(8,128)} %get-tuple-element.20) | data formatting | bytes 31104 | tf_op jit(solution)/shard_map/slice | solution.py:16
  74.6 3.7 %collective-permute-start.2 = (f32[3,36,36,1]{2,1,3,0:T(8,128)S(1)}, f32[3,36,36,1]{2,1,3,0:T(8,128)S(1)}, u32[]{:S(2)}, u32[]{:S(2)}) collective-permute-start(f32[3,36,36,1]{2,1,3,0:T(8,128)S(1)} %copy.79), channel_id=1, source_target_pairs={{0,1},{1,2},{2,3},{3,4},{4,5},{5,6},{6,7},{8,9},{9,10},{10,11},{11... | collective-permute-start | bytes 46664 | tf_op jit(solution)/shard_map/ppermute | solution.py:19
  78.3 2.5 %copy.82 = f32[3,36,36,1]{2,1,3,0:T(8,128)S(1)} copy(f32[3,36,36,1]{3,2,1,0:T(8,128)} %get-tuple-element.21) | data formatting | bytes 31104 | tf_op jit(solution)/shard_map/slice | solution.py:15
  82.9 2.2 %copy.80 = f32[3,36,36,1]{3,2,1,0:T(8,128)} copy(f32[3,36,36,1]{2,1,3,0:T(8,128)S(1)} %collective-permute-done.2) | data formatting | bytes 31104 | tf_op jit(solution)/shard_map/ppermute | solution.py:19
  86.4 2.3 %copy.83 = f32[3,36,36,1]{3,2,1,0:T(8,128)} copy(f32[3,36,36,1]{2,1,3,0:T(8,128)S(1)} %collective-permute-done.3) | data formatting | bytes 31104 | tf_op jit(solution)/shard_map/ppermute | solution.py:21
  88.6 2.9 %fusion.49 = (f32[128]{0:T(128)S(1)}, f32[1,36,36,128]{3,2,1,0:T(8,128)S(1)}) fusion(f32[3,36,36,1]{3,2,1,0:T(8,128)} %copy.83, f32[3,36,36,128]{3,2,1,0:T(8,128)S(1)} %constant_dynamic-update-slice_fusion, f32[36,36]{1,0:T(8,128)S(1)} %get-tuple-element.34, f32[3,36,36,1]{3,2,1,0:T(8,128)} %copy.80, f32[36,36]{1,0:T(8,128)S(1)} %get-tuple-element.35, ...), kind=kLoop, calls=%fused_computation.114 | loop fusion | flops 2488192 | bytes 4697216 | tf_op jit(solution)/shard_map/reduce_sum | solution.py:64
  93.7 6.7 %collective-permute-start.5 = (f32[1,36,36,128]{3,2,1,0:T(8,128)S(1)}, f32[1,36,36,128]{3,2,1,0:T(8,128)S(1)}, u32[]{:S(2)}, u32[]{:S(2)}) collective-permute-start(f32[1,36,36,128]{3,2,1,0:T(8,128)S(1)} %subtract_multiply_fusion.1), channel_id=1, source_target_pairs={{8,0},{16,8},{24,16},{32,24},{40,32},{48,40},{56,48},{64,56},{72,6... | collective-permute-start | bytes 1990664 | tf_op jit(solution)/shard_map/ppermute | solution.py:21
  103.5 2.3 %scatter_custom_fusion.1 = f32[3,128]{0,1:T(8,128)S(1)} fusion(s32[512]{0:T(512)S(1)} %bitcast.66, f32[512,3]{1,0:T(8,128)S(1)} %copy.95, f32[]{:T(128)} %constant.53.clone.1), kind=kCustom, calls=%fused_computation.54 | custom fusion | flops 1536 | bytes 1540 | tf_op jit(solution)/shard_map/scatter-add | solution.py:114
  106.4 6.9 %collective-permute-done.4 = f32[1,36,36,128]{3,2,1,0:T(8,128)S(1)} collective-permute-done((f32[1,36,36,128]{3,2,1,0:T(8,128)S(1)}, f32[1,36,36,128]{3,2,1,0:T(8,128)S(1)}, u32[]{:S(2)}, u32[]{:S(2)}) %collective-permute-start.4) | collective-permute-done | bytes 663584 | tf_op jit(solution)/shard_map/ppermute | solution.py:19
  116.1 2.1 %fusion.51 = (f32[3,36,36,1]{3,2,1,0:T(8,128)}, f32[3,36,36,1]{3,2,1,0:T(8,128)S(1)}) fusion(f32[3,36,36,128]{3,2,1,0:T(8,128)S(1)} %pad_maximum_fusion), kind=kLoop, calls=%fused_computation.115 | loop fusion | bytes 62208 | tf_op jit(solution)/shard_map/slice | solution.py:16
  118.1 2.5 %copy.100 = f32[3,36,36,1]{2,1,3,0:T(8,128)S(1)} copy(f32[3,36,36,1]{3,2,1,0:T(8,128)} %get-tuple-element.18) | data formatting | bytes 31104
  120.7 4.3 %collective-permute-start.6 = (f32[3,36,36,1]{2,1,3,0:T(8,128)S(1)}, f32[3,36,36,1]{2,1,3,0:T(8,128)S(1)}, u32[]{:S(2)}, u32[]{:S(2)}) collective-permute-start(f32[3,36,36,1]{2,1,3,0:T(8,128)S(1)} %copy.100), channel_id=1, source_target_pairs={{0,1},{1,2},{2,3},{3,4},{4,5},{5,6},{6,7},{8,9},{9,10},{10,11},{11... | collective-permute-start | bytes 46664 | tf_op jit(solution)/shard_map/ppermute | solution.py:19
  132.4 3.1 %copy.88 = f32[3,36,36,1]{3,2,1,0:T(8,128)} copy(f32[3,36,36,1]{2,1,3,0:T(8,128)} %collective-permute-done.7) | data formatting | bytes 31104 | tf_op jit(solution)/shard_map/ppermute | solution.py:21
  135.5 3.2 %fusion.47 = (f32[128]{0:T(128)S(1)}, f32[1,36,36,128]{3,2,1,0:T(8,128)S(1)}) fusion(f32[1,36,36,128]{3,2,1,0:T(8,128)S(1)} %subtract_multiply_fusion.1, f32[3,36,36,1]{3,2,1,0:T(8,128)} %copy.88, f32[1,36,36,128]{3,2,1,0:T(8,128)} %copy-done.2, f32[1,36,36,128]{3,2,1,0:T(8,128)} %copy-done.1, f32[36,36]{1,0:T(8,128)S(1)} %get-tuple-element.34, ...), kind=kLoop, calls=%fused_computation.113 | loop fusion | flops 3151744 | bytes 2706560 | tf_op jit(solution)/shard_map/reduce_sum | solution.py:64
  140.5 11.9 %all-gather.1 = f32[272,1,128]{2,1,0:T(1,128)S(1)} all-gather(f32[34,1,128]{2,1,0:T(1,128)S(1)} %copy.90), channel_id=3, replica_groups=mesh['wave'=128,'ocean'=8] {'ocean'}, dimensions={0}, use_global_device_ids=true | all-gather | bytes 156672 | tf_op jit(solution)/shard_map/all_gather | solution.py:135
  154.2 3.7 %gather_fusion.1 = f32[512,34]{1,0:T(8,128)S(1)} fusion(f32[8,34,128]{1,2,0:T(8,128)S(1)} %copy.91, s32[512]{0:T(512)S(1)} %reshape.657), kind=kCustom, calls=%fused_computation.1 | custom fusion | bytes 143360 | tf_op jit(solution)/shard_map/vmap(jit(_take))/gather | solution.py:93
  158.0 5.5 %gather_fusion = f32[2048,34]{1,0:T(8,128)S(1)} fusion(f32[34,512]{0,1:T(8,128)S(1)} %bitcast.50, s32[2048]{0:T(1024)S(1)} %broadcast_clamp_fusion), kind=kCustom, calls=%fused_computation | custom fusion | bytes 565248 | tf_op jit(solution)/shard_map/jit(_take)/gather | solution.py:100
  (117 shorter events, 35.0 us)
Async XLA Ops:
  2.6 40.3 %copy-start.5 = (s32[4,512]{1,0:T(4,128)S(1)}, s32[4,512]{1,0:T(4,128)}, u32[]{:S(2)}) copy-start(s32[4,512]{1,0:T(4,128)} %param.13) | copy-start | bytes 24580
  2.6 40.4 %copy-start.14 = (f32[2,1,128]{2,1,0:T(1,128)S(1)}, f32[2,1,128]{2,1,0:T(1,128)}, u32[]{:S(2)}) copy-start(f32[2,1,128]{2,1,0:T(1,128)} %param.9) | copy-start | bytes 3076
  2.7 40.4 %copy-start.17 = (s32[1,128]{1,0:T(1,128)S(1)}, s32[1,128]{1,0:T(1,128)}, u32[]{:S(2)}) copy-start(s32[1,128]{1,0:T(1,128)} %param.10) | copy-start | bytes 1540
  2.7 40.4 %copy-start.6 = (s32[8,64]{1,0:T(8,128)S(1)}, s32[8,64]{1,0:T(8,128)}, u32[]{:S(2)}) copy-start(s32[8,64]{1,0:T(8,128)} %param.11) | copy-start | bytes 6148
  2.7 56.4 %copy-start.18 = (s32[8,1]{0,1:T(1,128)S(1)}, s32[8,1]{0,1:T(1,128)}, u32[]{:S(2)}) copy-start(s32[8,1]{0,1:T(1,128)} %param.12) | copy-start | bytes 100
  2.7 64.2 %collective-permute-start = (f32[1,36,36,128]{3,2,1,0:T(8,128)}, f32[1,36,36,128]{3,2,1,0:T(8,128)}, u32[]{:S(2)}, u32[]{:S(2)}) collective-permute-start(f32[1,36,36,128]{3,2,1,0:T(8,128)} %copy.75), channel_id=1, source_target_pairs={{0,8},{8,16},{16,24},{24,32},{32,40},{40,48},{48,56},{56,64},{64,7... | collective-permute-start | bytes 1990664 | tf_op jit(solution)/shard_map/ppermute | solution.py:19
  6.8 61.3 %collective-permute-start.1 = (f32[1,36,36,128]{3,2,1,0:T(8,128)}, f32[1,36,36,128]{3,2,1,0:T(8,128)}, u32[]{:S(2)}, u32[]{:S(2)}) collective-permute-start(f32[1,36,36,128]{3,2,1,0:T(8,128)} %copy.75), channel_id=1, source_target_pairs={{8,0},{16,8},{24,16},{32,24},{40,32},{48,40},{56,48},{64,56},{72,6... | collective-permute-start | bytes 1990664 | tf_op jit(solution)/shard_map/ppermute | solution.py:21
  24.9 43.2 %copy-start = (f32[1,36,36,128]{3,0,2,1:T(1,128)S(1)}, f32[1,36,36,128]{3,0,2,1:T(1,128)}, u32[]{:S(2)}) copy-start(f32[1,36,36,128]{3,0,2,1:T(1,128)} %param.8) | copy-start | bytes 1990660
  37.6 64.3 %all-to-all-start = ((f32[8,1,192]{2,1,0:T(1,128)}), f32[8,1,192]{2,1,0:T(1,128)S(1)}, u32[]{:S(2)}, u32[]{:S(2)}) async-start(f32[8,1,192]{2,1,0:T(1,128)} %reshape.704), calls=%async_computation | async-start | bytes 16384 | tf_op jit(solution)/shard_map/all_to_all | solution.py:150
  43.0 48.6 %copy-start.8 = (f32[128]{0:T(128)}, f32[128]{0:T(128)S(1)}, u32[]{:S(2)}) copy-start(f32[128]{0:T(128)S(1)} %convert_bitcast_fusion) | copy-start | bytes 1540
  66.8 24.7 %copy-start.12 = (f32[36]{0:T(128)}, f32[36]{0:T(128)S(1)}, u32[]{:S(2)}) copy-start(f32[36]{0:T(128)S(1)} %fusion.38) | copy-start | bytes 436
  74.6 8.3 %collective-permute-start.2 = (f32[3,36,36,1]{2,1,3,0:T(8,128)S(1)}, f32[3,36,36,1]{2,1,3,0:T(8,128)S(1)}, u32[]{:S(2)}, u32[]{:S(2)}) collective-permute-start(f32[3,36,36,1]{2,1,3,0:T(8,128)S(1)} %copy.79), channel_id=1, source_target_pairs={{0,1},{1,2},{2,3},{3,4},{4,5},{5,6},{6,7},{8,9},{9,10},{10,11},{11... | collective-permute-start | bytes 46664 | tf_op jit(solution)/shard_map/ppermute | solution.py:19
  80.8 5.5 %collective-permute-start.3 = (f32[3,36,36,1]{2,1,3,0:T(8,128)S(1)}, f32[3,36,36,1]{2,1,3,0:T(8,128)S(1)}, u32[]{:S(2)}, u32[]{:S(2)}) collective-permute-start(f32[3,36,36,1]{2,1,3,0:T(8,128)S(1)} %copy.82), channel_id=1, source_target_pairs={{1,0},{2,1},{3,2},{4,3},{5,4},{6,5},{7,6},{9,8},{10,9},{11,10},{12... | collective-permute-start | bytes 46664 | tf_op jit(solution)/shard_map/ppermute | solution.py:21
  82.8 8.8 %copy-start.10 = (f32[36]{0:T(128)}, f32[36]{0:T(128)S(1)}, u32[]{:S(2)}) copy-start(f32[36]{0:T(128)S(1)} %fusion.39) | copy-start | bytes 436
  91.8 21.5 %collective-permute-start.4 = (f32[1,36,36,128]{3,2,1,0:T(8,128)S(1)}, f32[1,36,36,128]{3,2,1,0:T(8,128)S(1)}, u32[]{:S(2)}, u32[]{:S(2)}) collective-permute-start(f32[1,36,36,128]{3,2,1,0:T(8,128)S(1)} %subtract_multiply_fusion.1), channel_id=1, source_target_pairs={{0,8},{8,16},{16,24},{24,32},{32,40},{40,48},{48,56},{56,64},{64,7... | collective-permute-start | bytes 1990664 | tf_op jit(solution)/shard_map/ppermute | solution.py:19
  93.7 21.3 %collective-permute-start.5 = (f32[1,36,36,128]{3,2,1,0:T(8,128)S(1)}, f32[1,36,36,128]{3,2,1,0:T(8,128)S(1)}, u32[]{:S(2)}, u32[]{:S(2)}) collective-permute-start(f32[1,36,36,128]{3,2,1,0:T(8,128)S(1)} %subtract_multiply_fusion.1), channel_id=1, source_target_pairs={{8,0},{16,8},{24,16},{32,24},{40,32},{48,40},{56,48},{64,56},{72,6... | collective-permute-start | bytes 1990664 | tf_op jit(solution)/shard_map/ppermute | solution.py:21
  120.7 9.2 %collective-permute-start.6 = (f32[3,36,36,1]{2,1,3,0:T(8,128)S(1)}, f32[3,36,36,1]{2,1,3,0:T(8,128)S(1)}, u32[]{:S(2)}, u32[]{:S(2)}) collective-permute-start(f32[3,36,36,1]{2,1,3,0:T(8,128)S(1)} %copy.100), channel_id=1, source_target_pairs={{0,1},{1,2},{2,3},{3,4},{4,5},{5,6},{6,7},{8,9},{9,10},{10,11},{11... | collective-permute-start | bytes 46664 | tf_op jit(solution)/shard_map/ppermute | solution.py:19
  126.6 5.8 %collective-permute-start.7 = (f32[3,36,36,1]{2,1,3,0:T(8,128)}, f32[3,36,36,1]{2,1,3,0:T(8,128)}, u32[]{:S(2)}, u32[]{:S(2)}) collective-permute-start(f32[3,36,36,1]{2,1,3,0:T(8,128)} %copy.101), channel_id=1, source_target_pairs={{1,0},{2,1},{3,2},{4,3},{5,4},{6,5},{7,6},{9,8},{10,9},{11,10},{12... | collective-permute-start | bytes 46664 | tf_op jit(solution)/shard_map/ppermute | solution.py:21
  135.5 3.2 %copy-start.13 = (f32[36]{0:T(128)S(1)}, f32[36]{0:T(128)}, u32[]{:S(2)}) copy-start(f32[36]{0:T(128)} %copy-done.12) | copy-start | bytes 436
  135.5 3.3 %copy-start.9 = (f32[128]{0:T(128)S(1)}, f32[128]{0:T(128)}, u32[]{:S(2)}) copy-start(f32[128]{0:T(128)} %copy-done.8) | copy-start | bytes 1540
  135.5 3.3 %copy-start.11 = (f32[36]{0:T(128)S(1)}, f32[36]{0:T(128)}, u32[]{:S(2)}) copy-start(f32[36]{0:T(128)} %copy-done.10) | copy-start | bytes 436
  135.5 3.6 %copy-start.3 = (f32[36,36,16]{1,2,0:T(8,128)S(1)}, f32[36,36,16]{1,2,0:T(8,128)}, u32[]{:S(2)}) copy-start(f32[36,36,16]{1,2,0:T(8,128)} %get-tuple-element.23) | copy-start | bytes 248836
  139.1 18.7 %copy-start.7 = (pred[8,64]{1,0:T(8,128)(4,1)S(1)}, pred[8,64]{1,0:T(8,128)(4,1)}, u32[]{:S(2)}) copy-start(pred[8,64]{1,0:T(8,128)(4,1)} %compare_and_fusion.1) | copy-start | bytes 1540
  154.1 9.4 %copy-start.4 = (f32[4,512]{1,0:T(4,128)S(1)}, f32[4,512]{1,0:T(4,128)}, u32[]{:S(2)}) copy-start(f32[4,512]{1,0:T(4,128)} %param.14) | copy-start | bytes 24580
  (4 other events, 5.8 us)
where the time goes:
time: 166 us; the launch traced here: 165 us
  starting transfers between devices  45.6 us (27%)
  local copies, waits for them, and re-layouts  44.7 us (27%)
  blocking collectives  32.5 us (20%)
  other arithmetic  27.5 us (17%)
  waiting for transfers between devices  11.6 us (7%)
  between operations  1.86 us (1%)
    ppermute x4, starting transfers between devices, with_halo(): lax.ppermute(head, axis, [((i + 1) % count, i) for i in range(ends)])  26.3 us
    ppermute x4, starting transfers between devices, with_halo(): lax.ppermute(tail, axis, [(i, (i + 1) % count) for i in range(ends)])  14.1 us
    unnamed x53, local copies, waits for them, and re-layouts  14.1 us
    all_gather x1, blocking collectives, per_device(): lax.all_gather(send_rows[None], 'ocean', axis=0, tiled=True)  13.5 us
    all_gather x1, blocking collectives, per_device(): lax.all_gather(flattened[None], 'ocean', axis=0, tiled=True)  11.9 us
    scatter-add x1, other arithmetic, spread_values(): jnp.zeros((3, slot_grand_sum), jnp.float32).at[:, picked.reshape(-1)]  11.6 us
    slice x3, local copies, waits for them, and re-layouts, with_halo(): lax.slice_in_dim(cells, cells.shape[dim] - width, cells.shape[dim], axis=...  7.3 us
    unnamed x1, blocking collectives  7.09 us
  transfers between devices with their start and end apart: 9, of which 4 were waited for; matrix products, arithmetic and copies ran while one was open for 27% of the time, Pallas kernels for 0%

commit v1 on v0

v1 whole, which is shorter than its diff:
```python
import functools

import jax
import jax.numpy as jnp
import ml_dtypes
import numpy as np
from jax import lax
from jax.experimental import pallas as pl
from jax.experimental.pallas import tpu as pltpu
from jax.sharding import PartitionSpec as P

ND = 36
NF = 36
FP = 40
DEPTHS = 16
CAP = 64
QUAD = 9
MESH = pl.DeviceIdType.MESH
F32 = jnp.float32
BF16 = jnp.bfloat16
HALVES = ((0, 16), (16, 20))
EDGE = QUAD * 2 * NF


def host_tables():
    angles = (np.arange(ND) + 0.5) * (2.0 * np.pi / ND)
    cosine, sines = np.cos(angles), np.sin(angles)
    frequency = np.arange(NF)
    speeds = 0.7 * 1.1 ** (-frequency)
    ratios = 1.1 ** (frequency - (NF - 1.0))
    kappas = 0.02 * 1.1 ** (2.0 * frequency)
    depths = 0.25 * np.arange(DEPTHS)
    kernel = np.sqrt(kappas)[:, None] * np.exp(-2.0 * kappas[:, None] * depths[None, :])
    return cosine, sines, speeds, ratios, kernel


def split_rows(values):
    high = values.astype(ml_dtypes.bfloat16)
    low = (values - high.astype(np.float64)).astype(ml_dtypes.bfloat16)
    return np.concatenate([high, low], 0).astype(np.float32)


def projection(scale):
    _, _, _, ratios, kernel = host_tables()
    table = np.zeros((80, 256))

    def put(row, group, values):
        table[row, group * FP : group * FP + NF] = values * scale / ND

    for depth in range(DEPTHS):
        k = kernel[:, depth]
        for side in (0, 1):
            put(16 * side + depth, side, k)
            put(16 * side + depth, 2 + side, k * ratios)
            put(40 + 16 * side + depth, side, 0.3 * k * ratios)
    for side in (0, 1):
        put(32 + side, 4 + side, ratios)
        put(72 + side, 2 + side, 0.3 * ratios * ratios)
    return split_rows(table)


def constants():
    cosine, sines, speeds, ratios, _ = host_tables()
    ac, an = np.abs(cosine), np.abs(sines)
    coef = np.zeros((ND, 16))
    for i, column in enumerate((ac, an, cosine * ac, sines * ac, cosine * an, sines * an, cosine, sines, ac + an)):
        coef[:, i] = column
    wide = np.zeros((4, FP, 128))
    for i, column in enumerate((speeds, ratios, cosine, sines)):
        wide[i, :36] = column[:, None]
    return (
        coef.astype(np.float32),
        wide.astype(np.float32),
        projection(np.ones(NF)),
        projection(speeds),
    )


def mxu(a, b, dims=(((1,), (0,)), ((), ()))):
    return lax.dot_general(a, b, dims, preferred_element_type=F32)


def split(x):
    high = x.astype(BF16)
    return high, (x - high.astype(F32)).astype(BF16)


def interval(
    strips,
    owners,
    opts,
    coef,
    spectra,
    flat,
    wind_hbm,
    mask_hbm,
    rows_hbm,
    count_hbm,
    pick_hbm,
    weight_hbm,
    current_hbm,
    wide_hbm,
    wown_hbm,
    wxy_hbm,
    forcing,
    back,
    e_v,
    ex_v,
    m_v,
    flat_v,
    edge_v,
    wind,
    mask,
    rows,
    count,
    pick,
    weight,
    current,
    wide,
    wown,
    wxy,
    drive,
    sx_v,
    xq,
    yq,
    oq,
    eq,
    xs,
    xr,
    ys,
    yr,
    ps,
    pr,
    rs,
    rr,
    fs,
    fr,
    ts,
    tr,
    m2,
    b2,
    car,
    local_sem,
    send_sem,
    recv_sem,
):
    w, o = lax.axis_index("wave"), lax.axis_index("ocean")
    xp, xm = (lax.rem(w + 1, strips), o), (lax.rem(w + strips - 1, strips), o)
    yp, ym = (w, lax.rem(o + 1, owners)), (w, lax.rem(o + owners - 1, owners))

    def peer(j):
        return (w, lax.rem(o + j, owners))

    barrier = pltpu.get_barrier_semaphore()
    for device in (xp, xm, *(peer(j) for j in range(1, owners))):
        pl.semaphore_signal(barrier, inc=1, device_id=device, device_id_type=MESH)

    loads = []
    for src, dst in (
        (spectra.at[:, :, 0, :], e_v),
        (wind_hbm, wind),
        (wide_hbm, wide),
        (flat, flat_v),
        (rows_hbm, rows),
        (count_hbm, count),
        (mask_hbm, mask),
        (pick_hbm, pick),
        (weight_hbm, weight),
        (current_hbm, current),
        (wxy_hbm, wxy),
        (wown_hbm, wown),
    ):
        cp = pltpu.make_async_copy(src, dst, local_sem.at[len(loads)])
        cp.start()
        loads.append(cp)

    used = [0]

    def send(src, dst, device):
        i = used[0]
        used[0] += 1
        cp = pltpu.make_async_remote_copy(
            src_ref=src, dst_ref=dst, send_sem=send_sem.at[i], recv_sem=recv_sem.at[i], device_id=device, device_id_type=MESH
        )
        cp.start()
        return cp

    left_in = jnp.where(w > 0, 1.0, 0.0).astype(F32)
    right_in = jnp.where(w < strips - 1, 1.0, 0.0).astype(F32)
    down_in = jnp.where(o > 0, 1.0, 0.0).astype(F32)
    up_in = jnp.where(o < owners - 1, 1.0, 0.0).astype(F32)
    lane = lax.broadcasted_iota(jnp.int32, (1, 128), 1)

    for ref in (xq, yq, oq):
        ref[...] = jnp.zeros(ref.shape, F32)
    eq[...] = jnp.zeros(eq.shape, F32)

    for cp in loads[:3]:
        cp.wait()
    s_all, r_all = wide[0, 0:NF, :], wide[1, 0:NF, :]
    sums = []
    for q in range(4):

        def gather_energy(i, acc, q=q):
            d = q * QUAD + i
            e = e_v[d]
            return acc[0] + e, acc[1] + coef[d, 0] * e, acc[2] + coef[d, 1] * e

        zero = jnp.zeros((NF, 128), F32)
        sums.append(lax.fori_loop(0, QUAD, gather_energy, (zero, zero, zero), unroll=3))

    def over_f(x):
        return jnp.sum(x, axis=0, keepdims=True)

    gc = [x[1] for x in sums]
    gn = [x[2] for x in sums]
    en_xp, en_xm = over_f(s_all * (gc[0] + gc[3])), over_f(s_all * (gc[1] + gc[2]))
    en_yp, en_ym = over_f(s_all * (gn[0] + gn[1])), over_f(s_all * (gn[2] + gn[3]))
    en_own = over_f(sums[0][0] + sums[1][0] + sums[2][0] + sums[3][0]) - (en_xp + en_xm + en_yp + en_ym)
    en_yp, en_ym = pltpu.roll(en_yp, 1, 1), pltpu.roll(en_ym, 127, 1)

    w0, w1 = wind[0], wind[1]
    row8 = lax.broadcasted_iota(jnp.int32, (8, 128), 0)

    def tile(energy):
        return jnp.where(row8 == 0, energy, jnp.where(row8 == 1, w0, w1))

    xs[0], xs[1] = tile(en_xp), tile(en_xm)

    pl.semaphore_wait(barrier, owners + 1)
    early_x = [send(xs.at[0], xr.at[0], xp), send(xs.at[1], xr.at[1], xm)]
    chunk = {}
    for q in (0, 2, 3, 1):
        part = pl.ds(q * QUAD, QUAD)
        chunk[q] = send(spectra.at[part, :, 0, :], ex_v.at[part], xp if q in (0, 3) else xm)

    for cp in loads[3:]:
        cp.wait()
    for side, last in ((0, 127), (1, 0)):
        pickup = jnp.where(lax.broadcasted_iota(jnp.int32, (16, 128), 1) == last, 1.0, 0.0).astype(BF16)
        high, low = split(flat_v[pl.ds(side * EDGE, EDGE), :])
        turned = (((1,), (1,)), ((), ()))
        ys[side, :, 0:128] = tile(en_yp if side == 0 else en_ym)
        ys[side, :, 128 : 128 + EDGE] = (mxu(pickup, high, turned) + mxu(pickup, low, turned))[0:8]
        ys[side, :, 128 + EDGE : 896] = jnp.zeros((8, 768 - EDGE), F32)
    early_y = [send(ys.at[0], yr.at[0], yp), send(ys.at[1], yr.at[1], ym)]

    lane8 = lax.broadcasted_iota(jnp.int32, (1, owners), 1)
    for j in range(owners):
        to = lax.rem(o + j, owners)
        picked = rows[pl.ds(to, 1), :]
        live = jnp.sum(jnp.where(lane8 == to, count[...], 0).astype(F32), axis=1, keepdims=True).astype(jnp.int32)
        both = jnp.concatenate([picked, picked], axis=1)
        rs[j] = jnp.where(row8 == 0, both, jnp.broadcast_to(live, (8, 128)))
    lists = {j: send(rs.at[j], rr.at[j], peer(j)) for j in range(1, owners)}
    rr[0] = rs[0]

    for j in range(owners):
        source = lax.rem(o + owners - j, owners)
        slots = lax.broadcasted_iota(jnp.int32, (CAP, opts), 0) + source * CAP
        total = jnp.zeros((CAP, opts), F32)
        for k in range(4):
            total = total + jnp.where(pick[k : k + 1, :] == slots, weight[k : k + 1, :], 0.0)
        high, low = split(total)
        m2[j, 0:CAP, :] = high
        m2[j, CAP : 2 * CAP, :] = low

    for cp in early_x + early_y:
        cp.wait_recv()
    ct, nt = wide[2, 0:NF, :], wide[3, 0:NF, :]

    def driving(a, b):
        return 0.1 * jnp.maximum(a * ct + b * nt, 0.0)

    drive[0] = driving(w0, w1)
    drive[1] = jnp.where(
        ct > 0, driving(xr[1, 1:2, :], xr[1, 2:3, :]), driving(xr[0, 1:2, :], xr[0, 2:3, :])
    )
    up0 = jnp.where(lane == 127, pltpu.roll(yr[1, 1:2, 0:128], 127, 1), pltpu.roll(w0, 127, 1))
    up1 = jnp.where(lane == 127, pltpu.roll(yr[1, 2:3, 0:128], 127, 1), pltpu.roll(w1, 127, 1))
    dn0 = jnp.where(lane == 0, pltpu.roll(yr[0, 1:2, 0:128], 1, 1), pltpu.roll(w0, 1, 1))
    dn1 = jnp.where(lane == 0, pltpu.roll(yr[0, 2:3, 0:128], 1, 1), pltpu.roll(w1, 1, 1))
    drive[2] = jnp.where(nt > 0, driving(up0, up1), driving(dn0, dn1))
    energy = (
        en_own
        + left_in * xr[0, 0:1, :]
        + right_in * xr[1, 0:1, :]
        + jnp.where(lane == 0, down_in * yr[0, 0:1, 0:128], en_yp)
        + jnp.where(lane == 127, up_in * yr[1, 0:1, 0:128], en_ym)
    ) * (1.0 / (ND * NF))
    damp = 0.3 * (energy / (energy + 1.0))
    sx_v[0] = s_all * left_in
    sx_v[1] = s_all * right_in

    for side, (last, inside, shift) in enumerate(((0, down_in, 1), (127, up_in, 127))):
        place = jnp.where(lax.broadcasted_iota(jnp.int32, (16, 128), 1) == last, 1.0, 0.0)
        place = jnp.where(lax.rem(lax.broadcasted_iota(jnp.int32, (16, 128), 0), 8) == 0, place, 0.0).astype(BF16)
        high, low = split(yr[side, :, 128 : 128 + EDGE] * inside)
        both = jnp.concatenate([high.astype(F32), low.astype(F32)], axis=0).astype(BF16)
        edge_v[side] = mxu(both, place, (((0,), (0,)), ((), ())))
        for half in (0, 1):
            for i in range(QUAD):
                d = side * 2 * QUAD + half * QUAD + i
                e = e_v[d]
                k = (half * QUAD + i) * NF
                behind = jnp.where(lane == last, edge_v[side, k : k + NF, :], pltpu.roll(e, shift, 1))
                m_v[d] = e + s_all * (coef[d, 1] * behind - coef[d, 8] * e)

    carried = current[...]
    ones = jnp.ones((1, opts), F32)
    c_high = carried.astype(BF16).astype(F32)
    none = jnp.zeros((5, opts), F32)
    car[...] = jnp.concatenate([c_high, ones, none, carried - c_high, jnp.zeros((6, opts), F32)], axis=0).astype(BF16)
    point = lax.broadcasted_iota(jnp.int32, (128, 128), 0)
    slot = lax.rem(lax.broadcasted_iota(jnp.int32, (1, 128), 1), CAP)
    for j in range(owners):
        if j:
            lists[j].wait_recv()
        hit = jnp.logical_and(rr[j, 0:1, :] == point, slot < rr[j, 1:2, :])
        matrix = mxu(jnp.where(hit, 1.0, 0.0).astype(BF16), m2[j])
        high, low = split(matrix)
        b2[j, 0:128, :] = high
        b2[j, 128:256, :] = low
        t = mxu(car[...], b2[j], (((1,), (1,)), ((), ())))
        ts[j] = t[0:8, 0:128] + t[8:16, 0:128] + t[0:8, 128:256] + t[8:16, 128:256]
    returns = {j: send(ts.at[j], tr.at[j], peer(owners - j)) for j in range(1, owners)}

    seen = set()
    for q in (0, 2, 3, 1):
        chunk[q].wait_recv()
        x_side, y_side = (0 if q in (0, 3) else 1), (0 if q in (0, 1) else 1)
        for low, n in HALVES:
            part = pl.ds(low, n)
            r = wide[1, part, :]
            sx = sx_v[x_side, part, :]

            def bins(i, acc, q=q, part=part, r=r, sx=sx):
                d = q * QUAD + i
                moved = m_v[d, part, :] + sx * (coef[d, 0] * ex_v[d, part, :])
                e = moved + moved * (r * (drive[0, pl.ds(d, 1), :] - damp))
                m_v[d, part, :] = e
                out = []
                for at, (a, kc, kn) in ((1, (0, 2, 3)), (2, (1, 4, 5))):
                    here = drive[at, pl.ds(d, 1), :]
                    e1 = e * here
                    e2 = e1 * here
                    a, kc, kn = coef[d, a], coef[d, kc], coef[d, kn]
                    out += [a * e, kc * e, kn * e, kc * e1, kn * e1, kc * e2, kn * e2]
                return tuple(x + y for x, y in zip(acc, out))

            acc = lax.fori_loop(0, QUAD, bins, (jnp.zeros((n, 128), F32),) * 14, unroll=3)
            for ref, side, kind, a in ((xq, x_side, 0, acc[:7]), (yq, y_side, 1, acc[7:])):
                col = pl.ds(side * 128, 128)
                parts = [a[1], a[2], a[3], a[4], a[3] + r * a[5], a[4] + r * a[6]]
                again = (kind, side, low) in seen
                seen.add((kind, side, low))
                for g, value in enumerate(parts):
                    at = pl.ds(g * FP + low, n)
                    ref[at, col] = ref[at, col] + value if again else value
                at = pl.ds(low, n)
                eq[2 * kind + side, at, :] = eq[2 * kind + side, at, :] + a[0] if again else a[0]

    sea = mask[...].astype(F32)

    def contract(table, x):
        high, low = split(x)
        both = table[...].astype(BF16)
        out = mxu(both, high)
        return out[0:80] + out[80:160] + mxu(both[0:80], low)

    def finish(value, energy_row):
        tail = value[32:40] + jnp.where(row8 == 2, energy_row, 0.0)
        return sea * jnp.concatenate([value[0:32], tail, value[40:80]], axis=0)

    s_pad = wide[0]
    out = contract(wxy, xq[...])
    for side in (0, 1):
        ps[side] = finish(out[:, side * 128 : side * 128 + 128], over_f(s_pad * eq[side]))
    sums_out = [send(ps.at[0], pr.at[0], xp), send(ps.at[1], pr.at[1], xm)]
    out = contract(wxy, yq[...])
    for side in (0, 1):
        value = finish(out[:, side * 128 : side * 128 + 128], over_f(s_pad * eq[2 + side]))
        ps[2 + side] = pltpu.roll(value, (1, 127)[side], 1)
    sums_out += [send(ps.at[2], pr.at[2], yp), send(ps.at[3], pr.at[3], ym)]

    e_own = []
    for low, n in HALVES:
        part = pl.ds(low, n)
        r, s = wide[1, part, :], wide[0, part, :]

        def own_bins(d, acc, part=part, s=s):
            e = m_v[d, part, :]
            e = e - s * (coef[d, 8] * e)
            here = drive[0, pl.ds(d, 1), :]
            e1 = e * here
            e2 = e1 * here
            kc, kn = coef[d, 6], coef[d, 7]
            out = (e, kc * e, kn * e, kc * e1, kn * e1, kc * e2, kn * e2)
            return tuple(x + y for x, y in zip(acc, out))

        a = lax.fori_loop(0, ND, own_bins, (jnp.zeros((n, 128), F32),) * 7, unroll=4)
        for g, value in enumerate([a[1], a[2], a[3], a[4], a[3] + r * a[5], a[4] + r * a[6]]):
            oq[pl.ds(g * FP + low, n), :] = value
        e_own.append(over_f(a[0]))
    total = finish(contract(wown, oq[...]), e_own[0] + e_own[1])

    for j in range(1, owners):
        returns[j].wait_recv()
    got = ts[0]
    for j in range(1, owners):
        got = got + tr[j]
    back[:, 0, :] = got[0:2] / jnp.maximum(got[2:3], 1.0)

    for cp in sums_out:
        cp.wait_recv()
    total = (
        total
        + left_in * pr[0]
        + right_in * pr[1]
        + jnp.where(lane == 0, down_in * pr[2], ps[2])
        + jnp.where(lane == 127, up_in * pr[3], ps[3])
    )
    energy = total[34:35] * (1.0 / (ND * NF))
    fs[...] = sea * (total[0:40] - (energy / (energy + 1.0)) * total[40:80])
    fields = {j: send(fs, fr.at[j], peer(j)) for j in range(1, owners)}

    acc = jnp.zeros((80, opts), F32)
    for j in range(owners):
        if j:
            fields[j].wait_recv()
        value = fr[j] if j else fs[...]
        high = value.astype(BF16).astype(F32)
        stack = jnp.concatenate([high, value - high], axis=0).astype(BF16)
        acc = acc + mxu(jnp.concatenate([stack, stack], axis=1), b2[j])
    forcing[...] = (acc[0:40] + acc[40:80])[0:34]

    for cp in (*early_x, *early_y, *chunk.values(), *lists.values(), *returns.values(), *sums_out, *fields.values()):
        cp.wait_send()


def per_device(spectra, surface_wind, water_mask, send_rows, send_count, pick_slot, pick_weight, ocean_current):
    strips, owners = lax.axis_size("wave"), lax.axis_size("ocean")
    opts = pick_slot.shape[1]
    coef, wide, wown, wxy = (jnp.asarray(x) for x in constants())
    anywhere = pl.BlockSpec(memory_space=pl.ANY)
    copies = 12 + 3 * (owners - 1)

    def f32(*shape):
        return pltpu.VMEM(shape, F32)

    def i32(*shape):
        return pltpu.VMEM(shape, jnp.int32)

    return pl.pallas_call(
        functools.partial(interval, strips, owners, opts),
        name="interval",
        out_shape=(
            jax.ShapeDtypeStruct((34, opts), F32),
            jax.ShapeDtypeStruct((2, 1, 128), F32),
        ),
        in_specs=[pl.BlockSpec(memory_space=pltpu.SMEM)] + [anywhere] * 12,
        out_specs=(pl.BlockSpec(memory_space=pltpu.VMEM),) * 2,
        scratch_shapes=[
            f32(ND, NF, 128),
            f32(ND, NF, 128),
            f32(ND, NF, 128),
            f32(ND * NF, 128),
            f32(2, EDGE, 128),
            f32(2, 1, 128),
            i32(1, 128),
            i32(owners, CAP),
            i32(1, owners),
            i32(4, opts),
            f32(4, opts),
            f32(2, opts),
            f32(4, FP, 128),
            f32(160, 256),
            f32(160, 256),
            f32(3, NF, 128),
            f32(2, NF, 128),
            f32(256, 256),
            f32(256, 256),
            f32(256, 128),
            f32(4, FP, 128),
            f32(2, 8, 128),
            f32(2, 8, 128),
            f32(2, 8, 896),
            f32(2, 8, 896),
            f32(4, 80, 128),
            f32(4, 80, 128),
            i32(owners, 8, 128),
            i32(owners, 8, 128),
            f32(40, 128),
            f32(owners, 40, 128),
            f32(owners, 8, 128),
            f32(owners, 8, 128),
            pltpu.VMEM((owners, 128, opts), BF16),
            pltpu.VMEM((owners, 256, opts), BF16),
            pltpu.VMEM((16, opts), BF16),
            pltpu.SemaphoreType.DMA((12,)),
            pltpu.SemaphoreType.DMA((copies,)),
            pltpu.SemaphoreType.DMA((copies,)),
        ],
        compiler_params=pltpu.CompilerParams(collective_id=0, has_side_effects=True, vmem_limit_bytes=60 << 20),
    )(
        coef,
        spectra.reshape(ND, NF, 1, 128),
        spectra.reshape(ND * NF, 128),
        surface_wind,
        water_mask,
        send_rows,
        send_count.reshape(1, owners),
        pick_slot,
        pick_weight,
        ocean_current,
        wide,
        wown,
        wxy,
    )


def solution(mesh):
    in_specs = (
        P("wave", None, None, "ocean"),
        P(None, "wave", "ocean"),
        P("wave", "ocean"),
        P(None, ("wave", "ocean")),
        P(None, ("wave", "ocean")),
        P(None, ("wave", "ocean")),
        P(None, ("wave", "ocean")),
        P(None, ("wave", "ocean")),
    )
    out_specs = (P(None, ("wave", "ocean")), P(None, "wave", "ocean"))
    return jax.shard_map(per_device, mesh=mesh, in_specs=in_specs, out_specs=out_specs, check_vma=False)
```

time: 166 us -> 47.7 us (0.29)
  the two profiles are of different devices: /device:TPU:33 before, /device:TPU:1 now
where the time goes in v1:
time: 47.7 us; the launch traced here: 47.4 us
  Pallas kernels  44.7 us (94%)
  local copies, waits for them, and re-layouts  2.09 us (4%)
  between operations  0.65 us (1%)
    pallas_call x1, Pallas kernels, per_device(): pl.pallas_call(functools.partial(interval, strips, owners, opts), name='i...  44.7 us
    unnamed x4, local copies, waits for them, and re-layouts  2.09 us

profile of v1, /device:TPU:1, one launch (start us, length us, event | category | flops | bytes accessed | tf_op | source)
XLA Modules:
  0.0 47.4 jit_solution(3678765990820691507)
XLA Ops:
  0.6 44.7 %interval.1 = (f32[34,512]{1,0:T(8,128)}, f32[2,1,128]{2,1,0:T(1,128)}) custom-call(f32[36,16]{1,0:T(8,128)} %constant.8.clone.coef, f32[36,36,1,128]{3,2,1,0:T(1,128)} %bitcast.3, f32[1296,128]{1,0:T(8,128)} %bitcast.4, f32[2,1,128]{2,1,0:T(1,128)} %wind_hbm.1, s32[1,128]{1,0:T(1,128)} %mask_hbm.1, s32[8,64]{1,0:T(8,128)} %rows_hbm.1, s32[1,8]{1,0:T(1,128)} %bitcast.5, ...), custom_call_target="tpu_custom_call" | custom-call | tf_op jit(solution)/shard_map/interval/pallas_call | solution.py:454
  45.3 0.0 copy-start
  45.3 1.5 %copy.16 = f32[34,512]{1,0:T(8,128)} copy(f32[34,512]{1,0:T(8,128)} %get-tuple-element.4) | data formatting | bytes 139264
  46.9 0.0 copy-done
  46.9 0.6 %copy.17 = f32[2,1,128]{2,1,0:T(1,128)} copy(f32[2,1,128]{2,1,0:T(1,128)S(1)} %copy-done) | data formatting | bytes 2048
Async XLA Ops:
  45.3 1.5 %copy-start = (f32[2,1,128]{2,1,0:T(1,128)S(1)}, f32[2,1,128]{2,1,0:T(1,128)}, u32[]{:S(2)}) copy-start(f32[2,1,128]{2,1,0:T(1,128)} %get-tuple-element.5) | copy-start | bytes 3076

commit v2 on v1

--- a/solution.py
+++ b/solution.py
@@ -19,6 +19,9 @@
 F32 = jnp.float32
 BF16 = jnp.bfloat16
 HALVES = ((0, 16), (16, 20))
+STEP = 3
+ROWS = 74
+CH = 34
 EDGE = QUAD * 2 * NF
 
 
@@ -89,7 +92,7 @@
     strips,
     owners,
     opts,
-    coef,
+    coef_hbm,
     spectra,
     flat,
     wind_hbm,
@@ -104,6 +107,7 @@
     wxy_hbm,
     forcing,
     back,
+    coef,
     e_v,
     ex_v,
     m_v,
@@ -120,11 +124,11 @@
     wown,
     wxy,
     drive,
-    sx_v,
+    ax_v,
+    ay_v,
     xq,
     yq,
     oq,
-    eq,
     xs,
     xr,
     ys,
@@ -151,13 +155,24 @@
     def peer(j):
         return (w, lax.rem(o + j, owners))
 
+    far_first = sorted(range(1, owners), key=lambda j: -min(j, owners - j))
+
+    has_left, has_right = w > 0, w < strips - 1
+
     barrier = pltpu.get_barrier_semaphore()
-    for device in (xp, xm, *(peer(j) for j in range(1, owners))):
+
+    def greet(device):
         pl.semaphore_signal(barrier, inc=1, device_id=device, device_id_type=MESH)
+
+    pl.when(has_right)(lambda: greet(xp))
+    pl.when(has_left)(lambda: greet(xm))
+    for j in far_first:
+        greet(peer(j))
 
     loads = []
     for src, dst in (
         (spectra.at[:, :, 0, :], e_v),
+        (coef_hbm, coef),
         (wind_hbm, wind),
         (wide_hbm, wide),
         (flat, flat_v),
@@ -176,26 +191,66 @@
 
     used = [0]
 
-    def send(src, dst, device):
+    def send(src, dst, device, there=None, back=None):
         i = used[0]
         used[0] += 1
         cp = pltpu.make_async_remote_copy(
             src_ref=src, dst_ref=dst, send_sem=send_sem.at[i], recv_sem=recv_sem.at[i], device_id=device, device_id_type=MESH
         )
-        cp.start()
-        return cp
-
-    left_in = jnp.where(w > 0, 1.0, 0.0).astype(F32)
-    right_in = jnp.where(w < strips - 1, 1.0, 0.0).astype(F32)
+
+        def under(condition, action):
+            if condition is None:
+                action()
+            else:
+                pl.when(condition)(action)
+
+        under(there, cp.start)
+        return lambda: under(back, cp.wait_recv), lambda: under(there, cp.wait_send)
+
+    def to_right(src, dst):
+        return send(src, dst, xp, has_right, has_left)
+
+    def to_left(src, dst):
+        return send(src, dst, xm, has_left, has_right)
+
     down_in = jnp.where(o > 0, 1.0, 0.0).astype(F32)
     up_in = jnp.where(o < owners - 1, 1.0, 0.0).astype(F32)
     lane = lax.broadcasted_iota(jnp.int32, (1, 128), 1)
 
     for ref in (xq, yq, oq):
         ref[...] = jnp.zeros(ref.shape, F32)
-    eq[...] = jnp.zeros(eq.shape, F32)
-
-    for cp in loads[:3]:
+    ax_v[...] = jnp.zeros(ax_v.shape, F32)
+    ay_v[...] = jnp.zeros(ay_v.shape, F32)
+
+    @pl.when(jnp.logical_not(has_left))
+    def _():
+        ex_v[0:QUAD] = jnp.zeros((QUAD, NF, 128), F32)
+        ex_v[3 * QUAD : ND] = jnp.zeros((QUAD, NF, 128), F32)
+        xr[0] = jnp.zeros((8, 128), F32)
+        pr[0] = jnp.zeros((ROWS, 128), F32)
+
+    @pl.when(jnp.logical_not(has_right))
+    def _():
+        ex_v[QUAD : 3 * QUAD] = jnp.zeros((2 * QUAD, NF, 128), F32)
+        xr[1] = jnp.zeros((8, 128), F32)
+        pr[1] = jnp.zeros((ROWS, 128), F32)
+
+    pl.semaphore_wait(barrier, owners - 1 + has_left.astype(jnp.int32) + has_right.astype(jnp.int32))
+    order = []
+    for i in range(0, QUAD, STEP):
+        order += [(0, i), (2, i)]
+    for i in range(0, QUAD, STEP):
+        order += [(3, i), (1, i)]
+    chunk = {}
+
+    def send_chunks(which):
+        for q, i in which:
+            part = pl.ds(q * QUAD + i, STEP)
+            chunk[q, i] = (to_right if q in (0, 3) else to_left)(spectra.at[part, :, 0, :], ex_v.at[part])
+
+    send_chunks(order[:4])
+
+    for cp in loads[:4]:
         cp.wait()
     s_all, r_all = wide[0, 0:NF, :], wide[1, 0:NF, :]
     sums = []
@@ -227,14 +282,10 @@
 
     xs[0], xs[1] = tile(en_xp), tile(en_xm)
 
-    pl.semaphore_wait(barrier, owners + 1)
-    early_x = [send(xs.at[0], xr.at[0], xp), send(xs.at[1], xr.at[1], xm)]
-    chunk = {}
-    for q in (0, 2, 3, 1):
-        part = pl.ds(q * QUAD, QUAD)
-        chunk[q] = send(spectra.at[part, :, 0, :], ex_v.at[part], xp if q in (0, 3) else xm)
-
-    for cp in loads[3:]:
+    early = [to_right(xs.at[0], xr.at[0]), to_left(xs.at[1], xr.at[1])]
+    send_chunks(order[4:])
+
+    for cp in loads[4:]:
         cp.wait()
     for side, last in ((0, 127), (1, 0)):
         pickup = jnp.where(lax.broadcasted_iota(jnp.int32, (16, 128), 1) == last, 1.0, 0.0).astype(BF16)
@@ -243,7 +294,7 @@
         ys[side, :, 0:128] = tile(en_yp if side == 0 else en_ym)
         ys[side, :, 128 : 128 + EDGE] = (mxu(pickup, high, turned) + mxu(pickup, low, turned))[0:8]
         ys[side, :, 128 + EDGE : 896] = jnp.zeros((8, 768 - EDGE), F32)
-    early_y = [send(ys.at[0], yr.at[0], yp), send(ys.at[1], yr.at[1], ym)]
+    early += [send(ys.at[0], yr.at[0], yp), send(ys.at[1], yr.at[1], ym)]
 
     lane8 = lax.broadcasted_iota(jnp.int32, (1, owners), 1)
     for j in range(owners):
@@ -252,7 +303,7 @@
         live = jnp.sum(jnp.where(lane8 == to, count[...], 0).astype(F32), axis=1, keepdims=True).astype(jnp.int32)
         both = jnp.concatenate([picked, picked], axis=1)
         rs[j] = jnp.where(row8 == 0, both, jnp.broadcast_to(live, (8, 128)))
-    lists = {j: send(rs.at[j], rr.at[j], peer(j)) for j in range(1, owners)}
+    lists = {j: send(rs.at[j], rr.at[j], peer(j)) for j in far_first}
     rr[0] = rs[0]
 
     for j in range(owners):
@@ -265,8 +316,8 @@
         m2[j, 0:CAP, :] = high
         m2[j, CAP : 2 * CAP, :] = low
 
-    for cp in early_x + early_y:
-        cp.wait_recv()
+    for arrive, _ in early:
+        arrive()
     ct, nt = wide[2, 0:NF, :], wide[3, 0:NF, :]
 
     def driving(a, b):
@@ -283,14 +334,12 @@
     drive[2] = jnp.where(nt > 0, driving(up0, up1), driving(dn0, dn1))
     energy = (
         en_own
-        + left_in * xr[0, 0:1, :]
-        + right_in * xr[1, 0:1, :]
+        + xr[0, 0:1, :]
+        + xr[1, 0:1, :]
         + jnp.where(lane == 0, down_in * yr[0, 0:1, 0:128], en_yp)
         + jnp.where(lane == 127, up_in * yr[1, 0:1, 0:128], en_ym)
     ) * (1.0 / (ND * NF))
     damp = 0.3 * (energy / (energy + 1.0))
-    sx_v[0] = s_all * left_in
-    sx_v[1] = s_all * right_in
 
     for side, (last, inside, shift) in enumerate(((0, down_in, 1), (127, up_in, 127))):
         place = jnp.where(lax.broadcasted_iota(jnp.int32, (16, 128), 1) == last, 1.0, 0.0)
@@ -315,7 +364,7 @@
     slot = lax.rem(lax.broadcasted_iota(jnp.int32, (1, 128), 1), CAP)
     for j in range(owners):
         if j:
-            lists[j].wait_recv()
+            lists[j][0]()
         hit = jnp.logical_and(rr[j, 0:1, :] == point, slot < rr[j, 1:2, :])
         matrix = mxu(jnp.where(hit, 1.0, 0.0).astype(BF16), m2[j])
         high, low = split(matrix)
@@ -323,42 +372,31 @@
         b2[j, 128:256, :] = low
         t = mxu(car[...], b2[j], (((1,), (1,)), ((), ())))
         ts[j] = t[0:8, 0:128] + t[8:16, 0:128] + t[0:8, 128:256] + t[8:16, 128:256]
-    returns = {j: send(ts.at[j], tr.at[j], peer(owners - j)) for j in range(1, owners)}
-
-    seen = set()
-    for q in (0, 2, 3, 1):
-        chunk[q].wait_recv()
+    returns = {j: send(ts.at[j], tr.at[j], peer(owners - j)) for j in far_first}
+
+    for q, first in order:
+        chunk[q, first][0]()
         x_side, y_side = (0 if q in (0, 3) else 1), (0 if q in (0, 1) else 1)
         for low, n in HALVES:
             part = pl.ds(low, n)
-            r = wide[1, part, :]
-            sx = sx_v[x_side, part, :]
-
-            def bins(i, acc, q=q, part=part, r=r, sx=sx):
-                d = q * QUAD + i
-                moved = m_v[d, part, :] + sx * (coef[d, 0] * ex_v[d, part, :])
-                e = moved + moved * (r * (drive[0, pl.ds(d, 1), :] - damp))
+            r, s = wide[1, part, :], wide[0, part, :]
+            acc = [ref[side, g, part, :] for ref, side in ((ax_v, x_side), (ay_v, y_side)) for g in range(7)]
+            for i in range(STEP):
+                d = q * QUAD + first + i
+                moved = m_v[d, part, :] + s * (coef[d, 0] * ex_v[d, part, :])
+                e = moved + moved * (r * (drive[0, d : d + 1, :] - damp))
                 m_v[d, part, :] = e
                 out = []
                 for at, (a, kc, kn) in ((1, (0, 2, 3)), (2, (1, 4, 5))):
-                    here = drive[at, pl.ds(d, 1), :]
+                    here = drive[at, d : d + 1, :]
                     e1 = e * here
                     e2 = e1 * here
                     a, kc, kn = coef[d, a], coef[d, kc], coef[d, kn]
                     out += [a * e, kc * e, kn * e, kc * e1, kn * e1, kc * e2, kn * e2]
-                return tuple(x + y for x, y in zip(acc, out))
-
-            acc = lax.fori_loop(0, QUAD, bins, (jnp.zeros((n, 128), F32),) * 14, unroll=3)
-            for ref, side, kind, a in ((xq, x_side, 0, acc[:7]), (yq, y_side, 1, acc[7:])):
-                col = pl.ds(side * 128, 128)
-                parts = [a[1], a[2], a[3], a[4], a[3] + r * a[5], a[4] + r * a[6]]
-                again = (kind, side, low) in seen
-                seen.add((kind, side, low))
-                for g, value in enumerate(parts):
-                    at = pl.ds(g * FP + low, n)
-                    ref[at, col] = ref[at, col] + value if again else value
-                at = pl.ds(low, n)
-                eq[2 * kind + side, at, :] = eq[2 * kind + side, at, :] + a[0] if again else a[0]
+                acc = [x + y for x, y in zip(acc, out)]
+            for ref, side, values in ((ax_v, x_side, acc[:7]), (ay_v, y_side, acc[7:])):
+                for g, value in enumerate(values):
+                    ref[side, g, part, :] = value
 
     sea = mask[...].astype(F32)
 
@@ -370,18 +408,25 @@
 
     def finish(value, energy_row):
         tail = value[32:40] + jnp.where(row8 == 2, energy_row, 0.0)
-        return sea * jnp.concatenate([value[0:32], tail, value[40:80]], axis=0)
-
-    s_pad = wide[0]
-    out = contract(wxy, xq[...])
-    for side in (0, 1):
-        ps[side] = finish(out[:, side * 128 : side * 128 + 128], over_f(s_pad * eq[side]))
-    sums_out = [send(ps.at[0], pr.at[0], xp), send(ps.at[1], pr.at[1], xm)]
-    out = contract(wxy, yq[...])
-    for side in (0, 1):
-        value = finish(out[:, side * 128 : side * 128 + 128], over_f(s_pad * eq[2 + side]))
-        ps[2 + side] = pltpu.roll(value, (1, 127)[side], 1)
-    sums_out += [send(ps.at[2], pr.at[2], yp), send(ps.at[3], pr.at[3], ym)]
+        return (sea * jnp.concatenate([value[0:32], tail, value[40:80]], axis=0))[0:ROWS]
+
+    s_pad, r_pad = wide[0], wide[1]
+    sums_out = []
+    for acc_v, q_v, at in ((ax_v, xq, 0), (ay_v, yq, 2)):
+        for side in (0, 1):
+            col = pl.ds(side * 128, 128)
+            for g in range(4):
+                q_v[g * FP : (g + 1) * FP, col] = acc_v[side, g + 1]
+            for g in (4, 5):
+                q_v[g * FP : (g + 1) * FP, col] = acc_v[side, g - 1] + r_pad * acc_v[side, g + 1]
+        out = contract(wxy, q_v[...])
+        for side in (0, 1):
+            value = finish(out[:, side * 128 : side * 128 + 128], over_f(s_pad * acc_v[side, 0]))
+            ps[at + side] = value if at == 0 else pltpu.roll(value, (1, 127)[side], 1)
+        if at == 0:
+            sums_out += [to_right(ps.at[0], pr.at[0]), to_left(ps.at[1], pr.at[1])]
+        else:
+            sums_out += [send(ps.at[2], pr.at[2], yp), send(ps.at[3], pr.at[3], ym)]
 
     e_own = []
     for low, n in HALVES:
@@ -405,45 +450,45 @@
     total = finish(contract(wown, oq[...]), e_own[0] + e_own[1])
 
     for j in range(1, owners):
-        returns[j].wait_recv()
+        returns[j][0]()
     got = ts[0]
     for j in range(1, owners):
         got = got + tr[j]
     back[:, 0, :] = got[0:2] / jnp.maximum(got[2:3], 1.0)
 
-    for cp in sums_out:
-        cp.wait_recv()
+    for arrive, _ in sums_out:
+        arrive()
     total = (
         total
-        + left_in * pr[0]
-        + right_in * pr[1]
+        + pr[0]
+        + pr[1]
         + jnp.where(lane == 0, down_in * pr[2], ps[2])
         + jnp.where(lane == 127, up_in * pr[3], ps[3])
     )
     energy = total[34:35] * (1.0 / (ND * NF))
-    fs[...] = sea * (total[0:40] - (energy / (energy + 1.0)) * total[40:80])
-    fields = {j: send(fs, fr.at[j], peer(j)) for j in range(1, owners)}
+    fs[...] = sea * (total[0:CH] - (energy / (energy + 1.0)) * total[40:ROWS])
+    fields = {j: send(fs, fr.at[j], peer(j)) for j in far_first}
 
     acc = jnp.zeros((80, opts), F32)
     for j in range(owners):
         if j:
-            fields[j].wait_recv()
-        value = fr[j] if j else fs[...]
+            fields[j][0]()
+        value = jnp.concatenate([fr[j] if j else fs[...], jnp.zeros((40 - CH, 128), F32)], axis=0)
         high = value.astype(BF16).astype(F32)
         stack = jnp.concatenate([high, value - high], axis=0).astype(BF16)
         acc = acc + mxu(jnp.concatenate([stack, stack], axis=1), b2[j])
     forcing[...] = (acc[0:40] + acc[40:80])[0:34]
 
-    for cp in (*early_x, *early_y, *chunk.values(), *lists.values(), *returns.values(), *sums_out, *fields.values()):
-        cp.wait_send()
+    for _, leave in (*early, *chunk.values(), *lists.values(), *returns.values(), *sums_out, *fields.values()):
+        leave()
 
 
 def per_device(spectra, surface_wind, water_mask, send_rows, send_count, pick_slot, pick_weight, ocean_current):
     strips, owners = lax.axis_size("wave"), lax.axis_size("ocean")
     opts = pick_slot.shape[1]
     coef, wide, wown, wxy = (jnp.asarray(x) for x in constants())
-    anywhere = pl.BlockSpec(memory_space=pl.ANY)
-    copies = 12 + 3 * (owners - 1)
+    anywhere = pl.BlockSpec(memory_space=pltpu.HBM)
+    copies = 8 + ND // STEP + 3 * (owners - 1)
 
     def f32(*shape):
         return pltpu.VMEM(shape, F32)
@@ -458,9 +503,10 @@
             jax.ShapeDtypeStruct((34, opts), F32),
             jax.ShapeDtypeStruct((2, 1, 128), F32),
         ),
-        in_specs=[pl.BlockSpec(memory_space=pltpu.SMEM)] + [anywhere] * 12,
+        in_specs=[anywhere] * 13,
         out_specs=(pl.BlockSpec(memory_space=pltpu.VMEM),) * 2,
         scratch_shapes=[
+            pltpu.SMEM((ND, 16), F32),
             f32(ND, NF, 128),
             f32(ND, NF, 128),
             f32(ND, NF, 128),
@@ -477,45 +523,50 @@
             f32(160, 256),
             f32(160, 256),
             f32(3, NF, 128),
-            f32(2, NF, 128),
+            f32(2, 7, FP, 128),
+            f32(2, 7, FP, 128),
             f32(256, 256),
             f32(256, 256),
             f32(256, 128),
-            f32(4, FP, 128),
             f32(2, 8, 128),
             f32(2, 8, 128),
             f32(2, 8, 896),
             f32(2, 8, 896),
-            f32(4, 80, 128),
-            f32(4, 80, 128),
+            f32(4, ROWS, 128),
+            f32(4, ROWS, 128),
             i32(owners, 8, 128),
             i32(owners, 8, 128),
-            f32(40, 128),
-            f32(owners, 40, 128),
+            f32(CH, 128),
+            f32(owners, CH, 128),
             f32(owners, 8, 128),
             f32(owners, 8, 128),
             pltpu.VMEM((owners, 128, opts), BF16),
             pltpu.VMEM((owners, 256, opts), BF16),
             pltpu.VMEM((16, opts), BF16),
-            pltpu.SemaphoreType.DMA((12,)),
+            pltpu.SemaphoreType.DMA((13,)),
             pltpu.SemaphoreType.DMA((copies,)),
             pltpu.SemaphoreType.DMA((copies,)),
         ],
-        compiler_params=pltpu.CompilerParams(collective_id=0, has_side_effects=True, vmem_limit_bytes=60 << 20),
+        compiler_params=pltpu.CompilerParams(collective_id=0, has_side_effects=True, vmem_limit_bytes=32 << 20),
     )(
-        coef,
-        spectra.reshape(ND, NF, 1, 128),
-        spectra.reshape(ND * NF, 128),
-        surface_wind,
-        water_mask,
-        send_rows,
-        send_count.reshape(1, owners),
-        pick_slot,
-        pick_weight,
-        ocean_current,
-        wide,
-        wown,
-        wxy,
+        *(
+            pltpu.with_memory_space_constraint(x, pltpu.HBM)
+            for x in (
+                coef,
+                spectra.reshape(ND, NF, 1, 128),
+                spectra.reshape(ND * NF, 128),
+                surface_wind,
+                water_mask,
+                send_rows,
+                send_count.reshape(1, owners),
+                pick_slot,
+                pick_weight,
+                ocean_current,
+                wide,
+                wown,
+                wxy,
+            )
+        )
     )
 
 

time: 47.7 us -> 41.5 us (0.87)
  the two profiles are of different devices: /device:TPU:1 before, /device:TPU:33 now
where the time goes in v2:
time: 41.5 us; the launch traced here: 41.3 us
  Pallas kernels  39.5 us (95%)
  local copies, waits for them, and re-layouts  1.2 us (3%)
  between operations  0.64 us (2%)
    pallas_call x1, Pallas kernels, per_device(): pl.pallas_call(functools.partial(interval, strips, owners, opts), name='i...  39.5 us
    unnamed x2, local copies, waits for them, and re-layouts  1.2 us

profile of v2, /device:TPU:33, one launch (start us, length us, event | category | flops | bytes accessed | tf_op | source)
XLA Modules:
  0.0 41.3 jit_solution(12181438333320757729)
XLA Ops:
  0.6 39.5 %interval.1 = (f32[34,512]{1,0:T(8,128)S(1)}, f32[2,1,128]{2,1,0:T(1,128)S(1)}) custom-call(f32[36,16]{1,0:T(8,128)} %constant.8.clone.coef_hbm, f32[36,36,1,128]{3,2,1,0:T(1,128)} %bitcast.3, f32[1296,128]{1,0:T(8,128)} %bitcast.4, f32[2,1,128]{2,1,0:T(1,128)} %wind_hbm.1, s32[1,128]{1,0:T(1,128)} %mask_hbm.1, s32[8,64]{1,0:T(8,128)} %rows_hbm.1, ...), custom_call_target="tpu_custom_call" | custom-call | tf_op jit(solution)/shard_map/interval/pallas_call | solution.py:499
  40.1 0.6 %copy.16 = f32[34,512]{1,0:T(8,128)} copy(f32[34,512]{1,0:T(8,128)S(1)} %get-tuple-element.4) | data formatting | bytes 139264
  40.7 0.6 %copy.17 = f32[2,1,128]{2,1,0:T(1,128)} copy(f32[2,1,128]{2,1,0:T(1,128)S(1)} %get-tuple-element.5) | data formatting | bytes 2048

commit v3 on v2

--- a/solution.py
+++ b/solution.py
@@ -126,8 +126,6 @@
     drive,
     ax_v,
     ay_v,
-    xq,
-    yq,
     oq,
     xs,
     xr,
@@ -135,15 +133,13 @@
     yr,
     ps,
     pr,
-    rs,
-    rr,
     fs,
     fr,
     ts,
     tr,
     m2,
-    b2,
-    car,
+    all_slots,
+    live_slots,
     local_sem,
     send_sem,
     recv_sem,
@@ -217,8 +213,7 @@
     up_in = jnp.where(o < owners - 1, 1.0, 0.0).astype(F32)
     lane = lax.broadcasted_iota(jnp.int32, (1, 128), 1)
 
-    for ref in (xq, yq, oq):
-        ref[...] = jnp.zeros(ref.shape, F32)
+    oq[...] = jnp.zeros(oq.shape, F32)
     ax_v[...] = jnp.zeros(ax_v.shape, F32)
     ay_v[...] = jnp.zeros(ay_v.shape, F32)
 
@@ -235,22 +230,7 @@
         xr[1] = jnp.zeros((8, 128), F32)
         pr[1] = jnp.zeros((ROWS, 128), F32)
 
-    pl.semaphore_wait(barrier, owners - 1 + has_left.astype(jnp.int32) + has_right.astype(jnp.int32))
-    order = []
-    for i in range(0, QUAD, STEP):
-        order += [(0, i), (2, i)]
-    for i in range(0, QUAD, STEP):
-        order += [(3, i), (1, i)]
-    chunk = {}
-
-    def send_chunks(which):
-        for q, i in which:
-            part = pl.ds(q * QUAD + i, STEP)
-            chunk[q, i] = (to_right if q in (0, 3) else to_left)(spectra.at[part, :, 0, :], ex_v.at[part])
-
-    send_chunks(order[:4])
-
-    for cp in loads[:4]:
+    for cp in loads[:5]:
         cp.wait()
     s_all, r_all = wide[0, 0:NF, :], wide[1, 0:NF, :]
     sums = []
@@ -282,11 +262,6 @@
 
     xs[0], xs[1] = tile(en_xp), tile(en_xm)
 
-    early = [to_right(xs.at[0], xr.at[0]), to_left(xs.at[1], xr.at[1])]
-    send_chunks(order[4:])
-
-    for cp in loads[4:]:
-        cp.wait()
     for side, last in ((0, 127), (1, 0)):
         pickup = jnp.where(lax.broadcasted_iota(jnp.int32, (16, 128), 1) == last, 1.0, 0.0).astype(BF16)
         high, low = split(flat_v[pl.ds(side * EDGE, EDGE), :])
@@ -294,17 +269,31 @@
         ys[side, :, 0:128] = tile(en_yp if side == 0 else en_ym)
         ys[side, :, 128 : 128 + EDGE] = (mxu(pickup, high, turned) + mxu(pickup, low, turned))[0:8]
         ys[side, :, 128 + EDGE : 896] = jnp.zeros((8, 768 - EDGE), F32)
+    pl.semaphore_wait(barrier, owners - 1 + has_left.astype(jnp.int32) + has_right.astype(jnp.int32))
+    early = [to_right(xs.at[0], xr.at[0]), to_left(xs.at[1], xr.at[1])]
     early += [send(ys.at[0], yr.at[0], yp), send(ys.at[1], yr.at[1], ym)]
 
+    orders = [[(q, i) for q in side for i in range(0, QUAD, STEP)] for side in ((0, 3), (2, 1))]
+    chunk = {}
+    for pair in zip(*orders):
+        for (q, i), towards in zip(pair, (to_right, to_left)):
+            part = pl.ds(q * QUAD + i, STEP)
+            chunk[q, i] = towards(e_v.at[part], ex_v.at[part])
+
+    for cp in loads[5:]:
+        cp.wait()
+
     lane8 = lax.broadcasted_iota(jnp.int32, (1, owners), 1)
+    point = lax.broadcasted_iota(jnp.int32, (128, 128), 0)
+    slot = lax.rem(lane, CAP)
     for j in range(owners):
         to = lax.rem(o + j, owners)
         picked = rows[pl.ds(to, 1), :]
-        live = jnp.sum(jnp.where(lane8 == to, count[...], 0).astype(F32), axis=1, keepdims=True).astype(jnp.int32)
-        both = jnp.concatenate([picked, picked], axis=1)
-        rs[j] = jnp.where(row8 == 0, both, jnp.broadcast_to(live, (8, 128)))
-    lists = {j: send(rs.at[j], rr.at[j], peer(j)) for j in far_first}
-    rr[0] = rs[0]
+        number = jnp.sum(jnp.where(lane8 == to, count[...], 0).astype(F32), axis=1, keepdims=True).astype(jnp.int32)
+        hit = jnp.concatenate([picked, picked], axis=1) == point
+        at = pl.ds(j * 128, 128)
+        all_slots[:, at] = jnp.where(hit, 1.0, 0.0).astype(BF16)
+        live_slots[:, at] = jnp.where(jnp.logical_and(hit, slot < number), 1.0, 0.0).astype(BF16)
 
     for j in range(owners):
         source = lax.rem(o + owners - j, owners)
@@ -313,8 +302,8 @@
         for k in range(4):
             total = total + jnp.where(pick[k : k + 1, :] == slots, weight[k : k + 1, :], 0.0)
         high, low = split(total)
-        m2[j, 0:CAP, :] = high
-        m2[j, CAP : 2 * CAP, :] = low
+        m2[pl.ds(j * 128, CAP), :] = high
+        m2[pl.ds(j * 128 + CAP, CAP), :] = low
 
     for arrive, _ in early:
         arrive()
@@ -359,22 +348,33 @@
     ones = jnp.ones((1, opts), F32)
     c_high = carried.astype(BF16).astype(F32)
     none = jnp.zeros((5, opts), F32)
-    car[...] = jnp.concatenate([c_high, ones, none, carried - c_high, jnp.zeros((6, opts), F32)], axis=0).astype(BF16)
-    point = lax.broadcasted_iota(jnp.int32, (128, 128), 0)
-    slot = lax.rem(lax.broadcasted_iota(jnp.int32, (1, 128), 1), CAP)
+    car = jnp.concatenate([c_high, ones, none, carried - c_high, jnp.zeros((6, opts), F32)], axis=0).astype(BF16)
+    t = mxu(car, m2[...], (((1,), (1,)), ((), ())))
+    t = t[0:8] + t[8:16]
     for j in range(owners):
-        if j:
-            lists[j][0]()
-        hit = jnp.logical_and(rr[j, 0:1, :] == point, slot < rr[j, 1:2, :])
-        matrix = mxu(jnp.where(hit, 1.0, 0.0).astype(BF16), m2[j])
-        high, low = split(matrix)
-        b2[j, 0:128, :] = high
-        b2[j, 128:256, :] = low
-        t = mxu(car[...], b2[j], (((1,), (1,)), ((), ())))
-        ts[j] = t[0:8, 0:128] + t[8:16, 0:128] + t[0:8, 128:256] + t[8:16, 128:256]
+        part = t[:, j * 128 : j * 128 + 128]
+        ts[j] = part + pltpu.roll(part, CAP, 1)
     returns = {j: send(ts.at[j], tr.at[j], peer(owners - j)) for j in far_first}
 
-    for q, first in order:
+    sea = mask[...].astype(F32)
+    s_pad, r_pad = wide[0], wide[1]
+
+    def contract(table, x):
+        high, low = split(x)
+        both = table[...].astype(BF16)
+        out = mxu(both, high)
+        return out[0:80] + out[80:160] + mxu(both[0:80], low)
+
+    def finish(value, energy_row):
+        tail = value[32:40] + jnp.where(row8 == 2, energy_row, 0.0)
+        return (sea * jnp.concatenate([value[0:32], tail, value[40:80]], axis=0))[0:ROWS]
+
+    def project(acc_v, side):
+        sums = [acc_v[side, g] for g in range(7)]
+        parts = sums[1:5] + [sums[3] + r_pad * sums[5], sums[4] + r_pad * sums[6], jnp.zeros((16, 128), F32)]
+        return finish(contract(wxy, jnp.concatenate(parts, axis=0)), over_f(s_pad * sums[0]))
+
+    def advance(q, first):
         chunk[q, first][0]()
         x_side, y_side = (0 if q in (0, 3) else 1), (0 if q in (0, 1) else 1)
         for low, n in HALVES:
@@ -398,35 +398,15 @@
                 for g, value in enumerate(values):
                     ref[side, g, part, :] = value
 
-    sea = mask[...].astype(F32)
-
-    def contract(table, x):
-        high, low = split(x)
-        both = table[...].astype(BF16)
-        out = mxu(both, high)
-        return out[0:80] + out[80:160] + mxu(both[0:80], low)
-
-    def finish(value, energy_row):
-        tail = value[32:40] + jnp.where(row8 == 2, energy_row, 0.0)
-        return (sea * jnp.concatenate([value[0:32], tail, value[40:80]], axis=0))[0:ROWS]
-
-    s_pad, r_pad = wide[0], wide[1]
     sums_out = []
-    for acc_v, q_v, at in ((ax_v, xq, 0), (ay_v, yq, 2)):
-        for side in (0, 1):
-            col = pl.ds(side * 128, 128)
-            for g in range(4):
-                q_v[g * FP : (g + 1) * FP, col] = acc_v[side, g + 1]
-            for g in (4, 5):
-                q_v[g * FP : (g + 1) * FP, col] = acc_v[side, g - 1] + r_pad * acc_v[side, g + 1]
-        out = contract(wxy, q_v[...])
-        for side in (0, 1):
-            value = finish(out[:, side * 128 : side * 128 + 128], over_f(s_pad * acc_v[side, 0]))
-            ps[at + side] = value if at == 0 else pltpu.roll(value, (1, 127)[side], 1)
-        if at == 0:
-            sums_out += [to_right(ps.at[0], pr.at[0]), to_left(ps.at[1], pr.at[1])]
-        else:
-            sums_out += [send(ps.at[2], pr.at[2], yp), send(ps.at[3], pr.at[3], ym)]
+    for side, towards in ((0, to_right), (1, to_left)):
+        for q, first in orders[side]:
+            advance(q, first)
+        ps[side] = project(ax_v, side)
+        sums_out.append(towards(ps.at[side], pr.at[side]))
+    for side, device in ((0, yp), (1, ym)):
+        ps[2 + side] = pltpu.roll(project(ay_v, side), (1, 127)[side], 1)
+        sums_out.append(send(ps.at[2 + side], pr.at[2 + side], device))
 
     e_own = []
     for low, n in HALVES:
@@ -451,9 +431,14 @@
 
     for j in range(1, owners):
         returns[j][0]()
-    got = ts[0]
-    for j in range(1, owners):
-        got = got + tr[j]
+    sums = []
+    for j in range(owners):
+        value = tr[j] if j else ts[0]
+        high = value.astype(BF16).astype(F32)
+        sums.append(jnp.where(lane < CAP, high, value - high))
+    sums = jnp.concatenate(sums, axis=1)
+    sums = jnp.concatenate([sums, jnp.zeros(sums.shape, F32)], axis=0).astype(BF16)
+    got = mxu(sums, all_slots[...], (((1,), (1,)), ((), ())))
     back[:, 0, :] = got[0:2] / jnp.maximum(got[2:3], 1.0)
 
     for arrive, _ in sums_out:
@@ -466,20 +451,39 @@
         + jnp.where(lane == 127, up_in * pr[3], ps[3])
     )
     energy = total[34:35] * (1.0 / (ND * NF))
-    fs[...] = sea * (total[0:CH] - (energy / (energy + 1.0)) * total[40:ROWS])
-    fields = {j: send(fs, fr.at[j], peer(j)) for j in far_first}
-
-    acc = jnp.zeros((80, opts), F32)
-    for j in range(owners):
+    value = sea * (total[0:CH] - (energy / (energy + 1.0)) * total[40:ROWS])
+
+    half = CH // 2
+    gap = jnp.zeros((24 - half, 128), F32)
+
+    def two_parts(x):
+        high = x.astype(BF16).astype(F32)
+        return jnp.concatenate([high, x - high], axis=0).astype(BF16)
+
+    out = mxu(two_parts(jnp.concatenate([value[0:half], gap, value[half:CH], gap], axis=0)), live_slots[...])
+    out = out[0:48] + out[48:96]
+    fields = {}
+    for j in far_first + [0]:
+        at = slice(j * 128, j * 128 + 128)
+        fs[j] = jnp.where(lane < CAP, out[0:half, at], out[24 : 24 + half, at])
         if j:
-            fields[j][0]()
-        value = jnp.concatenate([fr[j] if j else fs[...], jnp.zeros((40 - CH, 128), F32)], axis=0)
-        high = value.astype(BF16).astype(F32)
-        stack = jnp.concatenate([high, value - high], axis=0).astype(BF16)
-        acc = acc + mxu(jnp.concatenate([stack, stack], axis=1), b2[j])
-    forcing[...] = (acc[0:40] + acc[40:80])[0:34]
-
-    for _, leave in (*early, *chunk.values(), *lists.values(), *returns.values(), *sums_out, *fields.values()):
+            fields[j] = send(fs.at[j], fr.at[j], peer(j))
+
+    acc = jnp.zeros((96, opts), F32)
+    for j in range(0, owners, 2):
+        sides = []
+        for k in (j, j + 1):
+            if k:
+                fields[k][0]()
+            value = jnp.concatenate([fr[k] if k else fs[0], gap], axis=0)
+            other = pltpu.roll(value, CAP, 1)
+            sides.append(two_parts(jnp.concatenate([jnp.where(lane < CAP, value, other), jnp.where(lane < CAP, other, value)], axis=0)))
+        acc = acc + mxu(jnp.concatenate(sides, axis=1), m2[j * 128 : j * 128 + 256, :])
+    acc = acc[0:48] + acc[48:96]
+    forcing[0:half, :] = acc[0:half]
+    forcing[half:CH, :] = acc[24 : 24 + half]
+
+    for _, leave in (*early, *chunk.values(), *returns.values(), *sums_out, *fields.values()):
         leave()
 
 
@@ -488,7 +492,7 @@
     opts = pick_slot.shape[1]
     coef, wide, wown, wxy = (jnp.asarray(x) for x in constants())
     anywhere = pl.BlockSpec(memory_space=pltpu.HBM)
-    copies = 8 + ND // STEP + 3 * (owners - 1)
+    copies = 8 + ND // STEP + 2 * (owners - 1)
 
     def f32(*shape):
         return pltpu.VMEM(shape, F32)
@@ -525,8 +529,6 @@
             f32(3, NF, 128),
             f32(2, 7, FP, 128),
             f32(2, 7, FP, 128),
-            f32(256, 256),
-            f32(256, 256),
             f32(256, 128),
             f32(2, 8, 128),
             f32(2, 8, 128),
@@ -534,15 +536,13 @@
             f32(2, 8, 896),
             f32(4, ROWS, 128),
             f32(4, ROWS, 128),
-            i32(owners, 8, 128),
-            i32(owners, 8, 128),
-            f32(CH, 128),
-            f32(owners, CH, 128),
+            f32(owners, CH // 2, 128),
+            f32(owners, CH // 2, 128),
             f32(owners, 8, 128),
             f32(owners, 8, 128),
-            pltpu.VMEM((owners, 128, opts), BF16),
-            pltpu.VMEM((owners, 256, opts), BF16),
-            pltpu.VMEM((16, opts), BF16),
+            pltpu.VMEM((owners * 128, opts), BF16),
+            pltpu.VMEM((128, owners * 128), BF16),
+            pltpu.VMEM((128, owners * 128), BF16),
             pltpu.SemaphoreType.DMA((13,)),
             pltpu.SemaphoreType.DMA((copies,)),
             pltpu.SemaphoreType.DMA((copies,)),

time: 41.5 us -> 40.5 us (0.976)
  the two profiles are of different devices: /device:TPU:33 before, /device:TPU:48 now
where the time goes in v3:
time: 40.5 us; the launch traced here: 40.3 us
  Pallas kernels  38.5 us (95%)
  local copies, waits for them, and re-layouts  1.2 us (3%)
  between operations  0.64 us (2%)
    pallas_call x1, Pallas kernels, per_device(): pl.pallas_call(functools.partial(interval, strips, owners, opts), name='i...  38.5 us
    unnamed x2, local copies, waits for them, and re-layouts  1.2 us

profile of v3, /device:TPU:48, one launch (start us, length us, event | category | flops | bytes accessed | tf_op | source)
XLA Modules:
  0.0 40.3 jit_solution(3910801360228128176)
XLA Ops:
  0.6 38.5 %interval.1 = (f32[34,512]{1,0:T(8,128)S(1)}, f32[2,1,128]{2,1,0:T(1,128)S(1)}) custom-call(f32[36,16]{1,0:T(8,128)} %constant.8.clone.coef_hbm, f32[36,36,1,128]{3,2,1,0:T(1,128)} %bitcast.3, f32[1296,128]{1,0:T(8,128)} %bitcast.4, f32[2,1,128]{2,1,0:T(1,128)} %wind_hbm.1, s32[1,128]{1,0:T(1,128)} %mask_hbm.1, s32[8,64]{1,0:T(8,128)} %rows_hbm.1, ...), custom_call_target="tpu_custom_call" | custom-call | tf_op jit(solution)/shard_map/interval/pallas_call | solution.py:503
  39.1 0.6 %copy.16 = f32[34,512]{1,0:T(8,128)} copy(f32[34,512]{1,0:T(8,128)S(1)} %get-tuple-element.4) | data formatting | bytes 139264
  39.8 0.6 %copy.17 = f32[2,1,128]{2,1,0:T(1,128)} copy(f32[2,1,128]{2,1,0:T(1,128)S(1)} %get-tuple-element.5) | data formatting | bytes 2048

commit v4 on v3

--- a/solution.py
+++ b/solution.py
@@ -20,6 +20,7 @@
 BF16 = jnp.bfloat16
 HALVES = ((0, 16), (16, 20))
 STEP = 3
+AHEAD = 4
 ROWS = 74
 CH = 34
 EDGE = QUAD * 2 * NF
@@ -209,6 +210,12 @@
     def to_left(src, dst):
         return send(src, dst, xm, has_left, has_right)
 
+    def to_up(src, dst):
+        return send(src, dst, yp)
+
+    def to_down(src, dst):
+        return send(src, dst, ym)
+
     down_in = jnp.where(o > 0, 1.0, 0.0).astype(F32)
     up_in = jnp.where(o < owners - 1, 1.0, 0.0).astype(F32)
     lane = lax.broadcasted_iota(jnp.int32, (1, 128), 1)
@@ -230,7 +237,19 @@
         xr[1] = jnp.zeros((8, 128), F32)
         pr[1] = jnp.zeros((ROWS, 128), F32)
 
-    for cp in loads[:5]:
+    order = [(q, i) for pair in ((0, 2), (3, 1)) for i in range(0, QUAD, STEP) for q in pair]
+    chunk = {}
+
+    def send_chunks(which):
+        for q, i in which:
+            part = pl.ds(q * QUAD + i, STEP)
+            chunk[q, i] = (to_right if q in (0, 3) else to_left)(e_v.at[part], ex_v.at[part])
+
+    loads[0].wait()
+    pl.semaphore_wait(barrier, owners - 1 + has_left.astype(jnp.int32) + has_right.astype(jnp.int32))
+    send_chunks(order[:AHEAD])
+
+    for cp in loads[1:5]:
         cp.wait()
     s_all, r_all = wide[0, 0:NF, :], wide[1, 0:NF, :]
     sums = []
@@ -269,17 +288,10 @@
         ys[side, :, 0:128] = tile(en_yp if side == 0 else en_ym)
         ys[side, :, 128 : 128 + EDGE] = (mxu(pickup, high, turned) + mxu(pickup, low, turned))[0:8]
         ys[side, :, 128 + EDGE : 896] = jnp.zeros((8, 768 - EDGE), F32)
-    pl.semaphore_wait(barrier, owners - 1 + has_left.astype(jnp.int32) + has_right.astype(jnp.int32))
     early = [to_right(xs.at[0], xr.at[0]), to_left(xs.at[1], xr.at[1])]
-    early += [send(ys.at[0], yr.at[0], yp), send(ys.at[1], yr.at[1], ym)]
-
-    orders = [[(q, i) for q in side for i in range(0, QUAD, STEP)] for side in ((0, 3), (2, 1))]
-    chunk = {}
-    for pair in zip(*orders):
-        for (q, i), towards in zip(pair, (to_right, to_left)):
-            part = pl.ds(q * QUAD + i, STEP)
-            chunk[q, i] = towards(e_v.at[part], ex_v.at[part])
-
+    early += [to_up(ys.at[0], yr.at[0]), to_down(ys.at[1], yr.at[1])]
+
+    send_chunks(order[AHEAD:])
     for cp in loads[5:]:
         cp.wait()
 
@@ -369,10 +381,10 @@
         tail = value[32:40] + jnp.where(row8 == 2, energy_row, 0.0)
         return (sea * jnp.concatenate([value[0:32], tail, value[40:80]], axis=0))[0:ROWS]
 
-    def project(acc_v, side):
+    def columns(acc_v, side):
         sums = [acc_v[side, g] for g in range(7)]
         parts = sums[1:5] + [sums[3] + r_pad * sums[5], sums[4] + r_pad * sums[6], jnp.zeros((16, 128), F32)]
-        return finish(contract(wxy, jnp.concatenate(parts, axis=0)), over_f(s_pad * sums[0]))
+        return jnp.concatenate(parts, axis=0), over_f(s_pad * sums[0])
 
     def advance(q, first):
         chunk[q, first][0]()
@@ -398,15 +410,15 @@
                 for g, value in enumerate(values):
                     ref[side, g, part, :] = value
 
+    for q, first in order:
+        advance(q, first)
+    sides = [columns(ref, side) for ref in (ax_v, ay_v) for side in (0, 1)]
+    out = contract(wxy, jnp.concatenate([x for x, _ in sides], axis=1))
     sums_out = []
-    for side, towards in ((0, to_right), (1, to_left)):
-        for q, first in orders[side]:
-            advance(q, first)
-        ps[side] = project(ax_v, side)
-        sums_out.append(towards(ps.at[side], pr.at[side]))
-    for side, device in ((0, yp), (1, ym)):
-        ps[2 + side] = pltpu.roll(project(ay_v, side), (1, 127)[side], 1)
-        sums_out.append(send(ps.at[2 + side], pr.at[2 + side], device))
+    for at, (towards, shift) in enumerate(((to_right, 0), (to_left, 0), (to_up, 1), (to_down, 127))):
+        value = finish(out[:, at * 128 : at * 128 + 128], sides[at][1])
+        ps[at] = pltpu.roll(value, shift, 1) if shift else value
+        sums_out.append(towards(ps.at[at], pr.at[at]))
 
     e_own = []
     for low, n in HALVES:
@@ -487,6 +499,14 @@
         leave()
 
 
+def write_out(forcing, back, forcing_hbm, back_hbm, sem):
+    copies = [pltpu.make_async_copy(forcing, forcing_hbm, sem.at[0]), pltpu.make_async_copy(back, back_hbm, sem.at[1])]
+    for cp in copies:
+        cp.start()
+    for cp in copies:
+        cp.wait()
+
+
 def per_device(spectra, surface_wind, water_mask, send_rows, send_count, pick_slot, pick_weight, ocean_current):
     strips, owners = lax.axis_size("wave"), lax.axis_size("ocean")
     opts = pick_slot.shape[1]
@@ -500,7 +520,7 @@
     def i32(*shape):
         return pltpu.VMEM(shape, jnp.int32)
 
-    return pl.pallas_call(
+    results = pl.pallas_call(
         functools.partial(interval, strips, owners, opts),
         name="interval",
         out_shape=(
@@ -568,6 +588,17 @@
             )
         )
     )
+    return pl.pallas_call(
+        write_out,
+        name="write_out",
+        out_shape=(
+            jax.ShapeDtypeStruct((34, opts), F32),
+            jax.ShapeDtypeStruct((2, 1, 128), F32),
+        ),
+        in_specs=[pl.BlockSpec(memory_space=pltpu.VMEM)] * 2,
+        out_specs=(anywhere,) * 2,
+        scratch_shapes=[pltpu.SemaphoreType.DMA((2,))],
+    )(*(pltpu.with_memory_space_constraint(x, pltpu.VMEM) for x in results))
 
 
 def solution(mesh):

time: 40.5 us -> 39.9 us (0.985)
  the two profiles are of different devices: /device:TPU:48 before, /device:TPU:33 now
where the time goes in v4:
time: 39.9 us; the launch traced here: 39.8 us
  Pallas kernels  39.1 us (98%)
  between operations  0.64 us (2%)
    pallas_call x1, Pallas kernels, per_device(): pl.pallas_call(functools.partial(interval, strips, owners, opts), name='i...  38.5 us

profile of v4, /device:TPU:33, one launch (start us, length us, event | category | flops | bytes accessed | tf_op | source)
XLA Modules:
  0.0 39.8 jit_solution(8413499935963278834)
XLA Ops:
  0.6 38.5 %interval.1 = (f32[34,512]{1,0:T(8,128)S(1)}, f32[2,1,128]{2,1,0:T(1,128)S(1)}) custom-call(f32[36,16]{1,0:T(8,128)} %constant.8.clone.coef_hbm, f32[36,36,1,128]{3,2,1,0:T(1,128)} %bitcast.3, f32[1296,128]{1,0:T(8,128)} %bitcast.4, f32[2,1,128]{2,1,0:T(1,128)} %wind_hbm.1, s32[1,128]{1,0:T(1,128)} %mask_hbm.1, s32[8,64]{1,0:T(8,128)} %rows_hbm.1, ...), custom_call_target="tpu_custom_call" | custom-call | tf_op jit(solution)/shard_map/interval/pallas_call | solution.py:523
  39.1 0.7 %write_out.1 = (f32[34,512]{1,0:T(8,128)}, f32[2,1,128]{2,1,0:T(1,128)}) custom-call(f32[34,512]{1,0:T(8,128)S(1)} %get-tuple-element.4.forcing, f32[2,1,128]{2,1,0:T(1,128)S(1)} %get-tuple-element.5.back), custom_call_target="tpu_custom_call" | custom-call | tf_op jit(solution)/shard_map/write_out/pallas_call | solution.py:591

commit v5 on v4

--- a/solution.py
+++ b/solution.py
@@ -144,6 +144,7 @@
     local_sem,
     send_sem,
     recv_sem,
+    word_sem,
 ):
     w, o = lax.axis_index("wave"), lax.axis_index("ocean")
     xp, xm = (lax.rem(w + 1, strips), o), (lax.rem(w + strips - 1, strips), o)
@@ -163,8 +164,8 @@
 
     pl.when(has_right)(lambda: greet(xp))
     pl.when(has_left)(lambda: greet(xm))
-    for j in far_first:
-        greet(peer(j))
+    greet(yp)
+    greet(ym)
 
     loads = []
     for src, dst in (
@@ -246,8 +247,23 @@
             chunk[q, i] = (to_right if q in (0, 3) else to_left)(e_v.at[part], ex_v.at[part])
 
     loads[0].wait()
-    pl.semaphore_wait(barrier, owners - 1 + has_left.astype(jnp.int32) + has_right.astype(jnp.int32))
+    pl.semaphore_wait(barrier, 2 + has_left.astype(jnp.int32) + has_right.astype(jnp.int32))
     send_chunks(order[:AHEAD])
+
+    rounds = (owners - 2 + 1) // 2
+
+    def tell(r):
+        if r < rounds:
+            pl.semaphore_signal(word_sem.at[r, 0], inc=1, device_id=yp, device_id_type=MESH)
+            pl.semaphore_signal(word_sem.at[r, 1], inc=1, device_id=ym, device_id_type=MESH)
+
+    def hear(r):
+        if r < rounds:
+            pl.semaphore_wait(word_sem.at[r, 0], 1)
+            pl.semaphore_wait(word_sem.at[r, 1], 1)
+            tell(r + 1)
+
+    tell(0)
 
     for cp in loads[1:5]:
         cp.wait()
@@ -294,6 +310,8 @@
     send_chunks(order[AHEAD:])
     for cp in loads[5:]:
         cp.wait()
+
+    hear(0)
 
     lane8 = lax.broadcasted_iota(jnp.int32, (1, owners), 1)
     point = lax.broadcasted_iota(jnp.int32, (128, 128), 0)
@@ -307,6 +325,8 @@
         all_slots[:, at] = jnp.where(hit, 1.0, 0.0).astype(BF16)
         live_slots[:, at] = jnp.where(jnp.logical_and(hit, slot < number), 1.0, 0.0).astype(BF16)
 
+    hear(1)
+
     for j in range(owners):
         source = lax.rem(o + owners - j, owners)
         slots = lax.broadcasted_iota(jnp.int32, (CAP, opts), 0) + source * CAP
@@ -316,6 +336,20 @@
         high, low = split(total)
         m2[pl.ds(j * 128, CAP), :] = high
         m2[pl.ds(j * 128 + CAP, CAP), :] = low
+
+    carried = current[...]
+    ones = jnp.ones((1, opts), F32)
+    c_high = carried.astype(BF16).astype(F32)
+    none = jnp.zeros((5, opts), F32)
+    car = jnp.concatenate([c_high, ones, none, carried - c_high, jnp.zeros((6, opts), F32)], axis=0).astype(BF16)
+    t = mxu(car, m2[...], (((1,), (1,)), ((), ())))
+    t = t[0:8] + t[8:16]
+    for j in range(owners):
+        part = t[:, j * 128 : j * 128 + 128]
+        ts[j] = part + pltpu.roll(part, CAP, 1)
+    for r in range(2, rounds):
+        hear(r)
+    returns = {j: send(ts.at[j], tr.at[j], peer(owners - j)) for j in far_first}
 
     for arrive, _ in early:
         arrive()
@@ -355,18 +389,6 @@
                 k = (half * QUAD + i) * NF
                 behind = jnp.where(lane == last, edge_v[side, k : k + NF, :], pltpu.roll(e, shift, 1))
                 m_v[d] = e + s_all * (coef[d, 1] * behind - coef[d, 8] * e)
-
-    carried = current[...]
-    ones = jnp.ones((1, opts), F32)
-    c_high = carried.astype(BF16).astype(F32)
-    none = jnp.zeros((5, opts), F32)
-    car = jnp.concatenate([c_high, ones, none, carried - c_high, jnp.zeros((6, opts), F32)], axis=0).astype(BF16)
-    t = mxu(car, m2[...], (((1,), (1,)), ((), ())))
-    t = t[0:8] + t[8:16]
-    for j in range(owners):
-        part = t[:, j * 128 : j * 128 + 128]
-        ts[j] = part + pltpu.roll(part, CAP, 1)
-    returns = {j: send(ts.at[j], tr.at[j], peer(owners - j)) for j in far_first}
 
     sea = mask[...].astype(F32)
     s_pad, r_pad = wide[0], wide[1]
@@ -411,14 +433,24 @@
                     ref[side, g, part, :] = value
 
     for q, first in order:
-        advance(q, first)
-    sides = [columns(ref, side) for ref in (ax_v, ay_v) for side in (0, 1)]
-    out = contract(wxy, jnp.concatenate([x for x, _ in sides], axis=1))
+        if q in (0, 3):
+            advance(q, first)
     sums_out = []
-    for at, (towards, shift) in enumerate(((to_right, 0), (to_left, 0), (to_up, 1), (to_down, 127))):
-        value = finish(out[:, at * 128 : at * 128 + 128], sides[at][1])
-        ps[at] = pltpu.roll(value, shift, 1) if shift else value
-        sums_out.append(towards(ps.at[at], pr.at[at]))
+
+    def project(picks):
+        sides = [columns(ref, side) for ref, side, _, _ in picks]
+        out = contract(wxy, jnp.concatenate([x for x, _ in sides], axis=1))
+        for i, (ref, side, towards, shift) in enumerate(picks):
+            at = len(sums_out)
+            value = finish(out[:, i * 128 : i * 128 + 128], sides[i][1])
+            ps[at] = pltpu.roll(value, shift, 1) if shift else value
+            sums_out.append(towards(ps.at[at], pr.at[at]))
+
+    project([(ax_v, 0, to_right, 0)])
+    for q, first in order:
+        if q in (2, 1):
+            advance(q, first)
+    project([(ax_v, 1, to_left, 0), (ay_v, 0, to_up, 1), (ay_v, 1, to_down, 127)])
 
     e_own = []
     for low, n in HALVES:
@@ -566,6 +598,7 @@
             pltpu.SemaphoreType.DMA((13,)),
             pltpu.SemaphoreType.DMA((copies,)),
             pltpu.SemaphoreType.DMA((copies,)),
+            pltpu.SemaphoreType.REGULAR((max((owners - 1) // 2, 1), 2)),
         ],
         compiler_params=pltpu.CompilerParams(collective_id=0, has_side_effects=True, vmem_limit_bytes=32 << 20),
     )(

time: 39.9 us -> 38.5 us (0.965)
  the two profiles are of different devices: /device:TPU:33 before, /device:TPU:40 now
where the time goes in v5:
time: 38.5 us; the launch traced here: 38.3 us
  Pallas kernels  37.7 us (98%)
  between operations  0.64 us (2%)
    pallas_call x1, Pallas kernels, per_device(): pl.pallas_call(functools.partial(interval, strips, owners, opts), name='i...  37 us

profile of v5, /device:TPU:40, one launch (start us, length us, event | category | flops | bytes accessed | tf_op | source)
XLA Modules:
  0.0 38.3 jit_solution(16938732141041569732)
XLA Ops:
  0.6 37.0 %interval.1 = (f32[34,512]{1,0:T(8,128)S(1)}, f32[2,1,128]{2,1,0:T(1,128)S(1)}) custom-call(f32[36,16]{1,0:T(8,128)} %constant.8.clone.coef_hbm, f32[36,36,1,128]{3,2,1,0:T(1,128)} %bitcast.3, f32[1296,128]{1,0:T(8,128)} %bitcast.4, f32[2,1,128]{2,1,0:T(1,128)} %wind_hbm.1, s32[1,128]{1,0:T(1,128)} %mask_hbm.1, s32[8,64]{1,0:T(8,128)} %rows_hbm.1, ...), custom_call_target="tpu_custom_call" | custom-call | tf_op jit(solution)/shard_map/interval/pallas_call | solution.py:555
  37.6 0.7 %write_out.1 = (f32[34,512]{1,0:T(8,128)}, f32[2,1,128]{2,1,0:T(1,128)}) custom-call(f32[34,512]{1,0:T(8,128)S(1)} %get-tuple-element.4.forcing, f32[2,1,128]{2,1,0:T(1,128)S(1)} %get-tuple-element.5.back), custom_call_target="tpu_custom_call" | custom-call | tf_op jit(solution)/shard_map/write_out/pallas_call | solution.py:624

commit v6 on v5

--- a/solution.py
+++ b/solution.py
@@ -438,19 +438,18 @@
     sums_out = []
 
     def project(picks):
-        sides = [columns(ref, side) for ref, side, _, _ in picks]
+        sides = [columns(ref, side) for _, ref, side, _, _ in picks]
         out = contract(wxy, jnp.concatenate([x for x, _ in sides], axis=1))
-        for i, (ref, side, towards, shift) in enumerate(picks):
-            at = len(sums_out)
+        for i, (at, _, _, towards, shift) in enumerate(picks):
             value = finish(out[:, i * 128 : i * 128 + 128], sides[i][1])
             ps[at] = pltpu.roll(value, shift, 1) if shift else value
             sums_out.append(towards(ps.at[at], pr.at[at]))
 
-    project([(ax_v, 0, to_right, 0)])
+    project([(0, ax_v, 0, to_right, 0)])
     for q, first in order:
         if q in (2, 1):
             advance(q, first)
-    project([(ax_v, 1, to_left, 0), (ay_v, 0, to_up, 1), (ay_v, 1, to_down, 127)])
+    project([(2, ay_v, 0, to_up, 1), (3, ay_v, 1, to_down, 127), (1, ax_v, 1, to_left, 0)])
 
     e_own = []
     for low, n in HALVES:

time: 38.5 us -> 38.5 us (level)
  the two profiles are of different devices: /device:TPU:40 before, /device:TPU:41 now
where the time goes in v6:
time: 38.5 us; the launch traced here: 38.3 us
  Pallas kernels  37.7 us (98%)
  between operations  0.64 us (2%)
    pallas_call x1, Pallas kernels, per_device(): pl.pallas_call(functools.partial(interval, strips, owners, opts), name='i...  37 us

profile of v6, /device:TPU:41, one launch (start us, length us, event | category | flops | bytes accessed | tf_op | source)
XLA Modules:
  0.0 38.3 jit_solution(4947326763300362594)
XLA Ops:
  0.6 37.0 %interval.1 = (f32[34,512]{1,0:T(8,128)S(1)}, f32[2,1,128]{2,1,0:T(1,128)S(1)}) custom-call(f32[36,16]{1,0:T(8,128)} %constant.8.clone.coef_hbm, f32[36,36,1,128]{3,2,1,0:T(1,128)} %bitcast.3, f32[1296,128]{1,0:T(8,128)} %bitcast.4, f32[2,1,128]{2,1,0:T(1,128)} %wind_hbm.1, s32[1,128]{1,0:T(1,128)} %mask_hbm.1, s32[8,64]{1,0:T(8,128)} %rows_hbm.1, ...), custom_call_target="tpu_custom_call" | custom-call | tf_op jit(solution)/shard_map/interval/pallas_call | solution.py:554
  37.7 0.7 %write_out.1 = (f32[34,512]{1,0:T(8,128)}, f32[2,1,128]{2,1,0:T(1,128)}) custom-call(f32[34,512]{1,0:T(8,128)S(1)} %get-tuple-element.4.forcing, f32[2,1,128]{2,1,0:T(1,128)S(1)} %get-tuple-element.5.back), custom_call_target="tpu_custom_call" | custom-call | tf_op jit(solution)/shard_map/write_out/pallas_call | solution.py:623
